TPU v7x, 32 devices: a whole 2x2x4 slice. The times are simulated.
32 devices in a mesh: dp: 8 (over y, x, core), seq: 4 (over z).
Axes of the slice: x: 2, y: 2, z: 4, core: 2. Of those that a mesh axis runs over, the one named last changes fastest.
Arguments:
- tokens: bfloat16 [16, 1024, 1280], P('dp', 'seq'), may hold values from -6 to 6
- protein_lengths: int32 [16, 16], P('dp'), may hold values from 0 to 1024, as said below
- norm1_gain: bfloat16 [2, 1280], P(None, 'dp'), may hold values from 0.099609375 to 1.8984375
- norm1_bias: bfloat16 [2, 1280], P(None, 'dp'), may hold values from -3 to 3
- w_in: bfloat16 [2, 1280, 640], P(None, 'dp', 'seq'), may hold values from -0.15625 to 0.15625
- in_bias: bfloat16 [2, 640], P(None, 'dp'), may hold values from -3 to 3
- norm2_gain: bfloat16 [2, 640], P(None, 'dp'), may hold values from 0.099609375 to 1.8984375
- norm2_bias: bfloat16 [2, 640], P(None, 'dp'), may hold values from -3 to 3
- w_conv: bfloat16 [2, 5, 640, 640], P(None, None, 'dp', 'seq'), may hold values from -0.109375 to 0.109375
- conv_bias: bfloat16 [2, 640], P(None, 'dp'), may hold values from -3 to 3
- norm3_gain: bfloat16 [2, 640], P(None, 'dp'), may hold values from 0.099609375 to 1.8984375
- norm3_bias: bfloat16 [2, 640], P(None, 'dp'), may hold values from -3 to 3
- w_out: bfloat16 [2, 640, 1280], P(None, 'dp', 'seq'), may hold values from -0.3125 to 0.3125
- out_bias: bfloat16 [2, 1280], P(None, 'dp'), may hold values from -2 to 2
- cotangent: bfloat16 [16, 1024, 1280], P('dp', 'seq'), may hold values from -6 to 6
Outputs:
- output: bfloat16 [16, 1024, 1280], P('dp', 'seq')
- input_grad: float32 [16, 1024, 1280], P('dp', 'seq')
- grad_norm1_gain: float32 [2, 1280], P(None, 'dp')
- grad_norm1_bias: float32 [2, 1280], P(None, 'dp')
- grad_w_in: float32 [2, 1280, 640], P(None, 'dp', 'seq')
- grad_in_bias: float32 [2, 640], P(None, 'dp')
- grad_norm2_gain: float32 [2, 640], P(None, 'dp')
- grad_norm2_bias: float32 [2, 640], P(None, 'dp')
- grad_w_conv: float32 [2, 5, 640, 640], P(None, None, 'dp', 'seq')
- grad_conv_bias: float32 [2, 640], P(None, 'dp')
- grad_norm3_gain: float32 [2, 640], P(None, 'dp')
- grad_norm3_bias: float32 [2, 640], P(None, 'dp')
- grad_w_out: float32 [2, 640, 1280], P(None, 'dp', 'seq')
- grad_out_bias: float32 [2, 1280], P(None, 'dp')
Inputs may be any that keep to these rules, and one draw needn't show every extreme that they name: `protein_lengths`: in each row the nonzero lengths come first, each is 30 or more, and together they are at most 1024; in each aligned block of 2 rows, one row holds a protein that begins before position 256 and ends at the row's end.
All inputs are finite; a program needn't handle non-finite values.
Results may differ from a plain program's by a relative error of at most 0.014.
Values may be sent and summed in bfloat16 or wider, within the bound.
No kernel may reach another device: no remote copies, remote signals or barrier semaphores. Data moves between devices by JAX's collectives and lax.ppermute only.
A program may use at most 192 MiB of HBM per device.

v0:
```python
import jax
import jax.numpy as jnp
from jax import lax
from jax.sharding import PartitionSpec as P

KER = 5
FIRST_DILATION = 64
SECOND_DILATION = 128


epsilon = 1e-05


def extended(block, sides, width):
    for axis, dim in sides:
        count = lax.axis_size(axis)
        forward = [(i, i + 1) for i in range(count - 1)]
        backward = [(target, source) for source, target in forward]
        low = lax.ppermute(
            lax.slice_in_dim(block, block.shape[dim] - width, None, axis=dim), axis, forward
        )
        high = lax.ppermute(lax.slice_in_dim(block, 0, width, axis=dim), axis, backward)
        block = jnp.concatenate([low, block, high], axis=dim)
    return block


def norm_gelu(values, gain_vector, bias_vector):
    row_mean = jnp.mean(values, -1, keepdims=True)
    centred = values - row_mean
    spread = jnp.mean(centred * centred, -1, keepdims=True)
    return jax.nn.gelu(
        centred * lax.rsqrt(spread + epsilon) * gain_vector + bias_vector, approximate=True
    )


def kernel_tap_flags(lengths, token_positions, dilation_step):
    doc_ends = jnp.cumsum(lengths, axis=1)
    row_total = doc_ends[:, -1:]
    where_pos = token_positions[None, :, None]
    finished = doc_ends[:, None, :] <= where_pos
    doc_start = jnp.sum(jnp.where(finished, lengths[:, None, :], 0), axis=2)
    doc_stop = jnp.min(jnp.where(finished, row_total[:, :, None] + 1, doc_ends[:, None, :]), axis=2)
    is_live = token_positions[None, :] < row_total
    flag_list = []
    for tap_index in range(KER):
        target = token_positions[None, :] + (tap_index - KER // 2) * dilation_step
        flag_list.append(is_live & (target >= doc_start) & (target < doc_stop))
    return flag_list


def contract_rows(left_rows, right_rows):
    return lax.dot_general(
        left_rows, right_rows, (((0,), (0,)), ((), ())), preferred_element_type=jnp.float32
    )


def times_transpose(left_rows, weight):
    return lax.dot_general(
        left_rows, weight, (((1,), (1,)), ((), ())), preferred_element_type=jnp.float32
    )


def forward_taps(activations, flag_list, dilation_step):
    padded = extended(activations, (("seq", 1),), KER // 2 * dilation_step)
    seq_len = activations.shape[1]
    zero_value = jnp.zeros((), activations.dtype)
    pieces = [
        jnp.where(
            flag_list[tap_index][:, :, None],
            padded[:, tap_index * dilation_step : tap_index * dilation_step + seq_len],
            zero_value,
        )
        for tap_index in range(KER)
    ]
    return jnp.stack(pieces, axis=2).reshape(
        activations.shape[0] * seq_len, KER * activations.shape[2]
    )


def backward_taps(gradient, flag_list, dilation_step):
    padded = extended(gradient, (("seq", 1),), KER // 2 * dilation_step)
    seq_len = gradient.shape[1]
    zero_value = jnp.zeros((), gradient.dtype)
    pieces = []
    for tap_index in range(KER):
        mirror = KER - 1 - tap_index
        pieces.append(
            jnp.where(
                flag_list[mirror][:, :, None],
                padded[:, mirror * dilation_step : mirror * dilation_step + seq_len],
                zero_value,
            )
        )
    return jnp.stack(pieces, axis=2).reshape(gradient.shape[0] * seq_len, KER * gradient.shape[2])


def block_params_list(block_number, device_shards):
    (
        norm1_gain,
        norm1_bias,
        w_in,
        in_bias,
        norm2_gain,
        norm2_bias,
        w_conv,
        conv_bias,
        norm3_gain,
        norm3_bias,
        w_out,
        out_bias,
    ) = device_shards
    w_first = w_in[block_number]
    w_middle = w_conv[block_number]
    w_last = w_out[block_number]
    wide_vectors = jnp.stack(
        [norm1_gain[block_number], norm1_bias[block_number], out_bias[block_number]]
    )
    narrow_vectors = jnp.stack(
        [
            in_bias[block_number],
            norm2_gain[block_number],
            norm2_bias[block_number],
            conv_bias[block_number],
            norm3_gain[block_number],
            norm3_bias[block_number],
        ]
    )
    w_first, w_middle, w_last = (
        lax.all_gather(w_first, "seq", axis=1, tiled=True),
        lax.all_gather(w_middle, "seq", axis=2, tiled=True),
        lax.all_gather(w_last, "seq", axis=1, tiled=True),
    )
    w_first, w_middle, w_last, wide_vectors, narrow_vectors = (
        lax.all_gather(w_first, "dp", axis=0, tiled=True),
        lax.all_gather(w_middle, "dp", axis=1, tiled=True),
        lax.all_gather(w_last, "dp", axis=0, tiled=True),
        lax.all_gather(wide_vectors, "dp", axis=1, tiled=True),
        lax.all_gather(narrow_vectors, "dp", axis=1, tiled=True),
    )
    return (
        w_first,
        w_middle,
        w_last,
        wide_vectors.astype(jnp.float32),
        narrow_vectors.astype(jnp.float32),
    )


def block_forward_pass(inputs, weights, flag_list, dilation_step):
    w_first, w_middle, w_last, wide_vectors, narrow_vectors = weights
    row_count, seq_len, model_width = inputs.shape
    hidden = w_middle.shape[1]
    act_one = norm_gelu(
        inputs.reshape(row_count * seq_len, model_width), wide_vectors[0], wide_vectors[1]
    ).astype(jnp.bfloat16)
    projected = jnp.dot(act_one, w_first, preferred_element_type=jnp.float32) + narrow_vectors[0]
    act_two = norm_gelu(projected, narrow_vectors[1], narrow_vectors[2]).astype(jnp.bfloat16)
    tap_rows = forward_taps(act_two.reshape(row_count, seq_len, hidden), flag_list, dilation_step)
    conv_out = (
        jnp.dot(
            tap_rows, w_middle.reshape(KER * hidden, hidden), preferred_element_type=jnp.float32
        )
        + narrow_vectors[3]
    )
    act_three = norm_gelu(conv_out, narrow_vectors[4], narrow_vectors[5]).astype(jnp.bfloat16)
    branch = jnp.dot(act_three, w_last, preferred_element_type=jnp.float32) + wide_vectors[2]
    output = inputs + branch.reshape(row_count, seq_len, model_width)
    return (output, (act_one, projected, tap_rows, conv_out, act_three))


def backward_block(inputs, upstream, weights, flag_list, dilation_step):
    w_first, w_middle, w_last, wide_vectors, narrow_vectors = weights
    unused_slot, kept_values = block_forward_pass(inputs, weights, flag_list, dilation_step)
    act_one, projected, tap_rows, conv_out, act_three = kept_values
    row_count, seq_len, model_width = inputs.shape
    hidden = w_middle.shape[1]
    token_count = row_count * seq_len
    grad_branch = upstream.reshape(token_count, model_width).astype(jnp.bfloat16)
    grad_last = contract_rows(act_three, grad_branch)
    grad_out_bias = jnp.sum(grad_branch.astype(jnp.float32), axis=0)
    grad_three = times_transpose(grad_branch, w_last)
    unused_slot, pull_three = jax.vjp(norm_gelu, conv_out, narrow_vectors[4], narrow_vectors[5])
    grad_conv, grad_gain_three, grad_bias_three = pull_three(grad_three)
    grad_conv = grad_conv.astype(jnp.bfloat16)
    grad_conv_bias = jnp.sum(grad_conv.astype(jnp.float32), axis=0)
    grad_middle = contract_rows(tap_rows, grad_conv).reshape(KER, hidden, hidden)
    flipped = jnp.transpose(w_middle, (0, 2, 1)).reshape(KER * hidden, hidden)
    grad_two = jnp.dot(
        backward_taps(grad_conv.reshape(row_count, seq_len, hidden), flag_list, dilation_step),
        flipped,
        preferred_element_type=jnp.float32,
    )
    unused_slot, pull_two = jax.vjp(norm_gelu, projected, narrow_vectors[1], narrow_vectors[2])
    grad_projected, grad_gain_two, grad_bias_two = pull_two(grad_two)
    grad_projected = grad_projected.astype(jnp.bfloat16)
    grad_in_bias = jnp.sum(grad_projected.astype(jnp.float32), axis=0)
    grad_first = contract_rows(act_one, grad_projected)
    grad_one = times_transpose(grad_projected, w_first)
    unused_slot, pull_one = jax.vjp(
        norm_gelu, inputs.reshape(token_count, model_width), wide_vectors[0], wide_vectors[1]
    )
    grad_inputs, grad_gain_one, grad_bias_one = pull_one(grad_one)
    result = upstream + grad_inputs.reshape(row_count, seq_len, model_width)
    wide_grads = jnp.stack([grad_gain_one, grad_bias_one, grad_out_bias])
    narrow_grads = jnp.stack(
        [
            grad_in_bias,
            grad_gain_two,
            grad_bias_two,
            grad_conv_bias,
            grad_gain_three,
            grad_bias_three,
        ]
    )
    return (result, (grad_first, grad_middle, grad_last, wide_grads, narrow_grads))


def reduce_grads(block_grads):
    grad_first, grad_middle, grad_last, wide_grads, narrow_grads = block_grads
    wide_grads, narrow_grads = lax.psum((wide_grads, narrow_grads), "seq")
    grad_first, grad_middle, grad_last, wide_grads, narrow_grads = (
        lax.psum_scatter(grad_first, "dp", scatter_dimension=0, tiled=True),
        lax.psum_scatter(grad_middle, "dp", scatter_dimension=1, tiled=True),
        lax.psum_scatter(grad_last, "dp", scatter_dimension=0, tiled=True),
        lax.psum_scatter(wide_grads, "dp", scatter_dimension=1, tiled=True),
        lax.psum_scatter(narrow_grads, "dp", scatter_dimension=1, tiled=True),
    )
    grad_first, grad_middle, grad_last = (
        lax.psum_scatter(
            grad_first.astype(jnp.bfloat16), "seq", scatter_dimension=1, tiled=True
        ).astype(jnp.float32),
        lax.psum_scatter(
            grad_middle.astype(jnp.bfloat16), "seq", scatter_dimension=2, tiled=True
        ).astype(jnp.float32),
        lax.psum_scatter(
            grad_last.astype(jnp.bfloat16), "seq", scatter_dimension=1, tiled=True
        ).astype(jnp.float32),
    )
    return (grad_first, grad_middle, grad_last, wide_grads, narrow_grads)


def local(
    tokens,
    protein_lengths,
    norm1_gain,
    norm1_bias,
    w_in,
    in_bias,
    norm2_gain,
    norm2_bias,
    w_conv,
    conv_bias,
    norm3_gain,
    norm3_bias,
    w_out,
    out_bias,
    cotangent,
):
    device_shards = (
        norm1_gain,
        norm1_bias,
        w_in,
        in_bias,
        norm2_gain,
        norm2_bias,
        w_conv,
        conv_bias,
        norm3_gain,
        norm3_bias,
        w_out,
        out_bias,
    )
    seq_len = tokens.shape[1]
    token_positions = lax.axis_index("seq") * seq_len + jnp.arange(seq_len, dtype=jnp.int32)
    early_tap_flags = kernel_tap_flags(protein_lengths, token_positions, FIRST_DILATION)
    later_tap_flags = kernel_tap_flags(protein_lengths, token_positions, SECOND_DILATION)
    hidden_before_blocks = tokens.astype(jnp.float32)
    hidden_after_first, unused_slot = block_forward_pass(
        hidden_before_blocks, block_params_list(0, device_shards), early_tap_flags, FIRST_DILATION
    )
    hidden_after_second, unused_slot = block_forward_pass(
        hidden_after_first, block_params_list(1, device_shards), later_tap_flags, SECOND_DILATION
    )
    gradient_after_first, grads_late = backward_block(
        hidden_after_first,
        cotangent.astype(jnp.float32),
        block_params_list(1, device_shards),
        later_tap_flags,
        SECOND_DILATION,
    )
    reduced_late = reduce_grads(grads_late)
    grad_stream_zero, grads_early = backward_block(
        hidden_before_blocks,
        gradient_after_first,
        block_params_list(0, device_shards),
        early_tap_flags,
        FIRST_DILATION,
    )
    reduced_early = reduce_grads(grads_early)
    first_early, middle_early, last_early, wide_early, narrow_early = reduced_early
    first_late, middle_late, last_late, wide_late, narrow_late = reduced_late
    return (
        hidden_after_second.astype(jnp.bfloat16),
        grad_stream_zero,
        jnp.stack([wide_early[0], wide_late[0]]),
        jnp.stack([wide_early[1], wide_late[1]]),
        jnp.stack([first_early, first_late]),
        jnp.stack([narrow_early[0], narrow_late[0]]),
        jnp.stack([narrow_early[1], narrow_late[1]]),
        jnp.stack([narrow_early[2], narrow_late[2]]),
        jnp.stack([middle_early, middle_late]),
        jnp.stack([narrow_early[3], narrow_late[3]]),
        jnp.stack([narrow_early[4], narrow_late[4]]),
        jnp.stack([narrow_early[5], narrow_late[5]]),
        jnp.stack([last_early, last_late]),
        jnp.stack([wide_early[2], wide_late[2]]),
    )


def solution(mesh):
    placed = (
        P("dp", "seq", None),
        P("dp", None),
        P(None, "dp"),
        P(None, "dp"),
        P(None, "dp", "seq"),
        P(None, "dp"),
        P(None, "dp"),
        P(None, "dp"),
        P(None, None, "dp", "seq"),
        P(None, "dp"),
        P(None, "dp"),
        P(None, "dp"),
        P(None, "dp", "seq"),
        P(None, "dp"),
        P("dp", "seq", None),
    )
    return jax.shard_map(
        local,
        mesh=mesh,
        in_specs=placed,
        out_specs=(
            P("dp", "seq", None),
            P("dp", "seq", None),
            P(None, "dp"),
            P(None, "dp"),
            P(None, "dp", "seq"),
            P(None, "dp"),
            P(None, "dp"),
            P(None, "dp"),
            P(None, None, "dp", "seq"),
            P(None, "dp"),
            P(None, "dp"),
            P(None, "dp"),
            P(None, "dp", "seq"),
            P(None, "dp"),
        ),
        check_vma=False,
    )
```

profile of v0, /device:TPU:17, one launch (start us, length us, event | category | flops | bytes accessed | tf_op | source)
XLA Modules:
  0.0 910.1 jit_solution(12157596605670620334)
XLA Ops:
  8.4 13.7 %all-gather = bf16[1,160,640]{1,0,2:T(2,128)(2,1)S(1)} all-gather(bf16[1,160,160]{1,0,2:T(2,128)(2,1)S(1)} %copy.249), channel_id=2, replica_groups=mesh['dp'=8,'seq'=4] {'seq'}, dimensions={2}, use_global_device_ids=true | all-gather | bytes 256000 | tf_op jit(solution)/shard_map/all_gather | solution.py:129
  23.9 21.9 %all-gather.2 = bf16[1,5,80,640]{2,1,0,3:T(8,128)(2,1)S(1)} all-gather(bf16[1,5,80,160]{2,1,0,3:T(8,128)(2,1)S(1)} %copy.250), channel_id=4, replica_groups=mesh['dp'=8,'seq'=4] {'seq'}, dimensions={3}, use_global_device_ids=true | all-gather | bytes 640000 | tf_op jit(solution)/shard_map/all_gather | solution.py:130
  47.7 12.9 %all-gather.4 = bf16[1,80,1280]{1,0,2:T(2,128)(2,1)S(1)} all-gather(bf16[1,80,320]{1,0,2:T(2,128)(2,1)S(1)} %copy.251), channel_id=6, replica_groups=mesh['dp'=8,'seq'=4] {'seq'}, dimensions={2}, use_global_device_ids=true | all-gather | bytes 256000 | tf_op jit(solution)/shard_map/all_gather | solution.py:131
  61.9 13.7 %all-gather.6 = bf16[1,160,640]{1,0,2:T(2,128)(2,1)S(1)} all-gather(bf16[1,160,160]{1,0,2:T(2,128)(2,1)S(1)} %copy.252), channel_id=8, replica_groups=mesh['dp'=8,'seq'=4] {'seq'}, dimensions={2}, use_global_device_ids=true | all-gather | bytes 256000 | tf_op jit(solution)/shard_map/all_gather | solution.py:129
  77.3 18.5 %all-gather.8 = bf16[1,5,80,640]{2,1,0,3:T(8,128)(2,1)S(1)} all-gather(bf16[1,5,80,160]{2,1,0,3:T(8,128)(2,1)S(1)} %copy.253), channel_id=10, replica_groups=mesh['dp'=8,'seq'=4] {'seq'}, dimensions={3}, use_global_device_ids=true | all-gather | bytes 640000 | tf_op jit(solution)/shard_map/all_gather | solution.py:130
  98.4 20.7 %all-gather.12 = bf16[8,160,3]{1,2,0:T(4,128)(2,1)S(1)} all-gather(bf16[1,160,3]{1,2,0:T(4,128)(2,1)S(1)} %maximum_bitcast_fusion), channel_id=1, replica_groups=mesh['dp'=8,'seq'=4] {'dp'}, dimensions={0}, use_global_device_ids=true | all-gather | bytes 8640 | tf_op jit(solution)/shard_map/all_gather | solution.py:137
  137.6 8.9 all-gather.15
  188.4 12.8 %multiply_convert_fusion = bf16[512,1280]{1,0:T(8,128)(2,1)} fusion(f32[2,256,1280]{2,1,0:T(8,128)S(1)} %get-tuple-element.79, f32[1280]{0:T(1024)S(1)} %get-tuple-element.40, f32[1280]{0:T(1024)S(1)} %get-tuple-element.38, f32[512]{0:T(512)S(1)} %rsqrt.75, f32[512]{0:T(512)S(1)} %bitcast.364), kind=kLoop, calls=%fused_computation.30 | loop fusion | flops 8519680 | bytes 3946496 | tf_op jit(solution)/shard_map/convert_element_type | solution.py:155
  211.3 25.7 %all-gather.10 = bf16[1,80,1280]{1,0,2:T(2,128)(2,1)} all-gather(bf16[1,80,320]{1,0,2:T(2,128)(2,1)S(1)} %copy.254), channel_id=12, replica_groups=mesh['dp'=8,'seq'=4] {'seq'}, dimensions={2}, use_global_device_ids=true | all-gather | bytes 256000 | tf_op jit(solution)/shard_map/all_gather | solution.py:131
  414.9 11.2 %reduce-scatter.45.cloned.1.call-done = f32[80,1280]{1,0:T(8,128)} async-done(((f32[640,1280]{1,0:T(8,128)}), f32[80,1280]{1,0:T(8,128)}) %reduce-scatter.45.cloned.1.call-update) | async-done | bytes 409616 | tf_op jit(solution)/shard_map/reduce_scatter | solution.py:224
  433.1 43.1 %reduce-scatter.37.cloned.1.call-done = f32[160,640]{1,0:T(8,128)} async-done(((f32[1280,640]{1,0:T(8,128)}), f32[160,640]{1,0:T(8,128)}) %reduce-scatter.37.cloned.1.call-update) | async-done | bytes 409616 | tf_op jit(solution)/shard_map/reduce_scatter | solution.py:222
  481.5 31.7 %reduce-scatter.67.cloned.1.call-done = f32[80,6]{1,0:T(8,128)} async-done(((f32[640,6]{1,0:T(8,128)}), f32[80,6]{1,0:T(8,128)}) %reduce-scatter.67.cloned.1.call-update) | async-done | bytes 1936
  514.0 36.7 %reduce-scatter.63.cloned.1.call-done = f32[160,3]{1,0:T(8,128)} async-done(((f32[1280,3]{1,0:T(8,128)}), f32[160,3]{1,0:T(8,128)}) %reduce-scatter.63.cloned.1.call-update) | async-done | bytes 1936
  551.7 36.7 %reduce-scatter.61.cloned.1.call-done = f32[160,3]{1,0:T(8,128)} async-done(((f32[1280,3]{1,0:T(8,128)}), f32[160,3]{1,0:T(8,128)}) %reduce-scatter.61.cloned.1.call-update) | async-done | bytes 1936
  589.4 35.7 %reduce-scatter.65.cloned.1.call-done = f32[80,6]{1,0:T(8,128)} async-done(((f32[640,6]{1,0:T(8,128)}), f32[80,6]{1,0:T(8,128)}) %reduce-scatter.65.cloned.1.call-update) | async-done | bytes 1936
  626.0 12.1 %all-reduce = (f32[3,160]{1,0:T(4,128)S(1)}, f32[3,160]{1,0:T(4,128)S(1)}, f32[6,80]{1,0:T(8,128)S(1)}, f32[6,80]{1,0:T(8,128)S(1)}) all-reduce(f32[3,160]{1,0:T(4,128)S(1)} %copy.244, f32[3,160]{1,0:T(4,128)S(1)} %copy.242, f32[6,80]{1,0:T(8,128)S(1)} %copy.248, f32[6,80]{1,0:T(8,128)S(1)} %copy.246), channel_id=1, replica_groups=mesh['dp'=8,'seq'=4] {'seq'}, use_global_device_ids=true, to_apply=%region_35.36 | all-reduce | flops 1920 | bytes 15360 | tf_op jit(solution)/shard_map/psum | solution.py:220
  638.1 61.4 %reduce-scatter.43.cloned.1.call-done = f32[5,80,640]{2,1,0:T(8,128)} async-done(((f32[5,640,640]{2,1,0:T(8,128)}), f32[5,80,640]{2,1,0:T(8,128)}) %reduce-scatter.43.cloned.1.call-update) | async-done | bytes 1024016 | tf_op jit(solution)/shard_map/reduce_scatter | solution.py:223
  707.1 66.7 %reduce-scatter.41.cloned.1.call-done = f32[5,80,640]{2,1,0:T(8,128)} async-done(((f32[5,640,640]{2,1,0:T(8,128)}), f32[5,80,640]{2,1,0:T(8,128)}) %reduce-scatter.41.cloned.1.call-update) | async-done | bytes 1024016 | tf_op jit(solution)/shard_map/reduce_scatter | solution.py:223
  779.7 13.2 %reduce-scatter.59.cloned.1.call-done = bf16[320,80]{1,0:T(8,128)(2,1)} async-done(((bf16[1280,80]{1,0:T(8,128)(2,1)}), bf16[320,80]{1,0:T(8,128)(2,1)}) %reduce-scatter.59.cloned.1.call-update) | async-done | bytes 51216
  793.9 19.6 %reduce-scatter.51.cloned.1.call-done = bf16[160,160]{1,0:T(8,128)(2,1)} async-done(((bf16[640,160]{1,0:T(8,128)(2,1)}), bf16[160,160]{1,0:T(8,128)(2,1)}) %reduce-scatter.51.cloned.1.call-update) | async-done | bytes 51216
  814.5 19.6 %reduce-scatter.57.cloned.1.call-done = bf16[320,80]{1,0:T(8,128)(2,1)} async-done(((bf16[1280,80]{1,0:T(8,128)(2,1)}), bf16[320,80]{1,0:T(8,128)(2,1)}) %reduce-scatter.57.cloned.1.call-update) | async-done | bytes 51216
  835.8 18.7 %reduce-scatter.49.cloned.1.call-done = bf16[160,160]{1,0:T(8,128)(2,1)} async-done(((bf16[640,160]{1,0:T(8,128)(2,1)}), bf16[160,160]{1,0:T(8,128)(2,1)}) %reduce-scatter.49.cloned.1.call-update) | async-done | bytes 51216
  856.3 20.8 %reduce-scatter.55.cloned.1.call-done = bf16[160,400]{1,0:T(8,128)(2,1)} async-done(((bf16[640,400]{1,0:T(8,128)(2,1)}), bf16[160,400]{1,0:T(8,128)(2,1)}) %reduce-scatter.55.cloned.1.call-update) | async-done | bytes 128016
  878.5 21.9 %reduce-scatter.53.cloned.1.call-done = bf16[160,400]{1,0:T(8,128)(2,1)} async-done(((bf16[640,400]{1,0:T(8,128)(2,1)}), bf16[160,400]{1,0:T(8,128)(2,1)}) %reduce-scatter.53.cloned.1.call-update) | async-done | bytes 128016
  (469 shorter events, 295.4 us)
Async XLA Ops:
  7.2 140.8 %all-gather.23.cloned.1.call-start = ((), (), s32[]{:S(2)}) async-start(), calls=%async_computation.22 | async-start | bytes 1843200 | tf_op jit(solution)/shard_map/all_gather | solution.py:134
  23.6 153.1 %all-gather.25.cloned.1.call-start = ((), (), s32[]{:S(2)}) async-start(), calls=%async_computation.23 | async-start | bytes 4608000 | tf_op jit(solution)/shard_map/all_gather | solution.py:135
  47.5 135.7 %all-gather.27.cloned.1.call-start = ((), (), s32[]{:S(2)}) async-start(), calls=%async_computation.24 | async-start | bytes 1843200 | tf_op jit(solution)/shard_map/all_gather | solution.py:136
  61.6 139.5 %all-gather.29.cloned.1.call-start = ((), (), s32[]{:S(2)}) async-start(), calls=%async_computation.25 | async-start | bytes 1843200 | tf_op jit(solution)/shard_map/all_gather | solution.py:134
  77.0 182.4 %all-gather.31.cloned.1.call-start = ((), (), s32[]{:S(2)}) async-start(), calls=%async_computation.26 | async-start | bytes 4608000 | tf_op jit(solution)/shard_map/all_gather | solution.py:135
  97.7 173.1 %all-gather.33.cloned.1.call-start = ((), (), s32[]{:S(2)}) async-start(), calls=%async_computation.27 | async-start | bytes 1843200 | tf_op jit(solution)/shard_map/all_gather | solution.py:136
  209.2 34.8 %collective-permute-start.2 = (bf16[2,256,640]{1,0,2:T(2,128)(2,1)S(1)}, bf16[2,256,640]{1,0,2:T(2,128)(2,1)}, u32[]{:S(2)}, u32[]{:S(2)}) collective-permute-start(bf16[2,256,640]{1,0,2:T(2,128)(2,1)S(1)} %copy.208), channel_id=1, source_target_pairs={{0,1},{1,2},{2,3},{4,5},{5,6},{6,7},{8,9},{9,10},{10,11},{12,13},{... | collective-permute-start | bytes 1966088 | tf_op jit(solution)/shard_map/ppermute | solution.py:19
  238.9 171.8 %reduce-scatter.47.cloned.1.call-start = ((), (), s32[]{:S(2)}) async-start(), calls=%async_computation.21 | async-start | bytes 3686400 | tf_op jit(solution)/shard_map/reduce_scatter | solution.py:224
  276.2 136.6 %reduce-scatter.39.cloned.1.call-start = ((), (), s32[]{:S(2)}) async-start(), calls=%async_computation.17 | async-start | bytes 3686400 | tf_op jit(solution)/shard_map/reduce_scatter | solution.py:222
  319.9 106.1 %reduce-scatter.45.cloned.1.call-start = ((), (), s32[]{:S(2)}) async-start(), calls=%async_computation.20 | async-start | bytes 3686400 | tf_op jit(solution)/shard_map/reduce_scatter | solution.py:224
  335.8 140.3 %reduce-scatter.37.cloned.1.call-start = ((), (), s32[]{:S(2)}) async-start(), calls=%async_computation.16 | async-start | bytes 3686400 | tf_op jit(solution)/shard_map/reduce_scatter | solution.py:222
  342.1 17.2 %collective-permute-start.6 = (bf16[2,128,640]{1,0,2:T(2,128)(2,1)}, bf16[2,128,640]{1,0,2:T(2,128)(2,1)}, u32[]{:S(2)}, u32[]{:S(2)}) collective-permute-start(bf16[2,128,640]{1,0,2:T(2,128)(2,1)} %get-tuple-element.83), channel_id=1, source_target_pairs={{1,0},{2,1},{3,2},{5,4},{6,5},{7,6},{9,8},{10,9},{11,10},{13,12},{... | collective-permute-start | bytes 983048 | tf_op jit(solution)/shard_map/ppermute | solution.py:22
  379.1 134.1 %reduce-scatter.67.cloned.1.call-start = ((), (), s32[]{:S(2)}) async-start(), calls=%async_computation.37 | async-start | bytes 368640
  380.2 170.5 %reduce-scatter.63.cloned.1.call-start = ((), (), s32[]{:S(2)}) async-start(), calls=%async_computation.35 | async-start | bytes 737280
  391.5 196.9 %reduce-scatter.61.cloned.1.call-start = ((), (), s32[]{:S(2)}) async-start(), calls=%async_computation.34 | async-start | bytes 737280
  392.7 232.4 %reduce-scatter.65.cloned.1.call-start = ((), (), s32[]{:S(2)}) async-start(), calls=%async_computation.36 | async-start | bytes 368640
  393.8 305.7 %reduce-scatter.43.cloned.1.call-start = ((), (), s32[]{:S(2)}) async-start(), calls=%async_computation.19 | async-start | bytes 9216000 | tf_op jit(solution)/shard_map/reduce_scatter | solution.py:223
  401.7 372.1 %reduce-scatter.41.cloned.1.call-start = ((), (), s32[]{:S(2)}) async-start(), calls=%async_computation.18 | async-start | bytes 9216000 | tf_op jit(solution)/shard_map/reduce_scatter | solution.py:223
  410.7 382.2 %reduce-scatter.59.cloned.1.call-start = ((), (), s32[]{:S(2)}) async-start(), calls=%async_computation.33 | async-start | bytes 409600
  412.7 400.8 %reduce-scatter.51.cloned.1.call-start = ((), (), s32[]{:S(2)}) async-start(), calls=%async_computation.29 | async-start | bytes 409600
  414.8 419.3 %reduce-scatter.57.cloned.1.call-start = ((), (), s32[]{:S(2)}) async-start(), calls=%async_computation.32 | async-start | bytes 409600
  428.0 426.6 %reduce-scatter.49.cloned.1.call-start = ((), (), s32[]{:S(2)}) async-start(), calls=%async_computation.28 | async-start | bytes 409600
  478.2 398.9 %reduce-scatter.55.cloned.1.call-start = ((), (), s32[]{:S(2)}) async-start(), calls=%async_computation.31 | async-start | bytes 819200
  703.6 196.8 %reduce-scatter.53.cloned.1.call-start = ((), (), s32[]{:S(2)}) async-start(), calls=%async_computation.30 | async-start | bytes 819200
  (95 other events, 759.2 us)
Sparse Core Ops, SparseCore 0:
  23.7 30.9 all-gather.22
  57.1 36.2 all-gather.24
  95.9 26.0 all-gather.26
  124.3 26.0 all-gather.28
  152.1 36.3 all-gather.30
  239.1 30.3 all-gather.32
  276.3 49.0 reduce-scatter.46
  328.8 46.8 reduce-scatter.38
  379.1 46.8 reduce-scatter.44
  429.3 46.8 reduce-scatter.36
  479.8 33.2 reduce-scatter.66
  516.1 34.5 reduce-scatter.62
  553.9 34.5 reduce-scatter.60
  591.3 33.7 reduce-scatter.64
  628.6 70.8 reduce-scatter.42
  703.5 70.3 reduce-scatter.40
  776.0 16.9 reduce-scatter.58
  795.1 18.4 reduce-scatter.50
  815.8 18.2 reduce-scatter.56
  836.2 18.2 reduce-scatter.48
  857.4 19.6 reduce-scatter.54
  879.4 20.9 reduce-scatter.52
where the time goes:
time: 926 us; the launch traced here: 910 us
  waiting for transfers between devices  452 us (49%)
  blocking collectives  165 us (18%)
  local copies, waits for them, and re-layouts  91.2 us (10%)
  matrix products  80.5 us (9%)
  other arithmetic  79.8 us (9%)
  starting transfers between devices  24.5 us (3%)
  between operations  16.5 us (2%)
    unnamed x32, waiting for transfers between devices  255 us
    reduce_scatter x2, waiting for transfers between devices, reduce_grads(): lax.psum_scatter(grad_middle, 'dp', scatter_dimension=1, tiled=True)  128 us
    unnamed x216, local copies, waits for them, and re-layouts  45.1 us
    reduce_scatter x2, waiting for transfers between devices, reduce_grads(): lax.psum_scatter(grad_first, 'dp', scatter_dimension=0, tiled=True)  43.2 us
    all_gather x2, blocking collectives, block_params_list(): lax.all_gather(w_middle, 'seq', axis=2, tiled=True)  40.5 us
    all_gather x2, blocking collectives, block_params_list(): lax.all_gather(w_last, 'seq', axis=1, tiled=True)  38.6 us
    all_gather x2, blocking collectives, block_params_list(): lax.all_gather(wide_vectors, 'dp', axis=1, tiled=True)  28.6 us
    dot_general x6, matrix products, contract_rows(): lax.dot_general(left_rows, right_rows, (((0,), (0,)), ((), ())), preferre...  27.9 us
  transfers between devices with their start and end apart: 30, of which 18 were waited for; matrix products, arithmetic and copies ran while one was open for 25% of the time, Pallas kernels for 0%

commit v1 on v0

--- a/solution.py
+++ b/solution.py
@@ -94,56 +94,96 @@
     return jnp.stack(pieces, axis=2).reshape(gradient.shape[0] * seq_len, KER * gradient.shape[2])
 
 
-def block_params_list(block_number, device_shards):
-    (
-        norm1_gain,
-        norm1_bias,
-        w_in,
-        in_bias,
-        norm2_gain,
-        norm2_bias,
-        w_conv,
-        conv_bias,
-        norm3_gain,
-        norm3_bias,
-        w_out,
-        out_bias,
-    ) = device_shards
-    w_first = w_in[block_number]
-    w_middle = w_conv[block_number]
-    w_last = w_out[block_number]
-    wide_vectors = jnp.stack(
-        [norm1_gain[block_number], norm1_bias[block_number], out_bias[block_number]]
-    )
-    narrow_vectors = jnp.stack(
+def shifted(block, step):
+    count = lax.axis_size("seq")
+    return lax.ppermute(block, "seq", [(i, (i + step) % count) for i in range(count)])
+
+
+def weight_pack(block_number, device_shards):
+    w_in, w_conv, w_out = (device_shards[i][block_number] for i in (2, 6, 10))
+    width = w_in.shape[1]
+    folds = w_out.shape[1] // width
+    pieces = [w_in, w_conv.reshape(-1, width)]
+    pieces += [w_out[:, i * width : (i + 1) * width] for i in range(folds)]
+    return jnp.concatenate(pieces, axis=0)
+
+
+def vector_pack(block_number, device_shards, width):
+    order = (0, 1, 11, 3, 4, 5, 7, 8, 9)
+    flat = jnp.concatenate([device_shards[i][block_number] for i in order])
+    rows = -(-flat.shape[0] // (16 * width)) * 16
+    return jnp.pad(flat, (0, rows * width - flat.shape[0])).reshape(rows, width)
+
+
+def seq_gathered(packed):
+    count = lax.axis_size("seq")
+    me = lax.axis_index("seq")
+    held = [packed] + [shifted(packed, step) for step in range(1, count)]
+    ring = jnp.stack(held[::-1] + held[::-1])
+    return lax.dynamic_slice_in_dim(ring, (count - 1 - me) % count, count, axis=0)
+
+
+def folded_columns(out_parts):
+    count, folds, depth, width = out_parts.shape
+    per_fold = count // folds
+    return (
+        out_parts.reshape(folds, per_fold, folds, depth, width)
+        .transpose(0, 3, 1, 2, 4)
+        .reshape(folds * depth, per_fold * folds * width)
+    )
+
+
+def unfolded_columns(out_rows, folds, count):
+    per_fold = count // folds
+    depth = out_rows.shape[0] // folds
+    width = out_rows.shape[1] // count
+    return (
+        out_rows.reshape(folds, depth, per_fold, folds, width)
+        .transpose(0, 2, 3, 1, 4)
+        .reshape(count, folds * depth, width)
+    )
+
+
+def gathered_params(block_number, device_shards):
+    w_in, w_conv, w_out = (device_shards[i][block_number] for i in (2, 6, 10))
+    first_rows = w_in.shape[0]
+    taps, middle_rows, width = w_conv.shape
+    folds = w_out.shape[1] // width
+    count = lax.axis_size("seq")
+    hidden = width * count
+    by_seq = seq_gathered(weight_pack(block_number, device_shards))
+    straight = first_rows + taps * middle_rows
+    upper = by_seq[:, :straight].transpose(1, 0, 2).reshape(straight, hidden)
+    lower = folded_columns(by_seq[:, straight:].reshape(count, folds, middle_rows, width))
+    vectors = vector_pack(block_number, device_shards, hidden)
+    whole = lax.all_gather(jnp.concatenate([upper, lower, vectors]), "dp")
+    parts = whole.shape[0]
+    w_first = whole[:, :first_rows].reshape(parts * first_rows, hidden)
+    w_middle = (
+        whole[:, first_rows:straight]
+        .reshape(parts, taps, middle_rows, hidden)
+        .transpose(1, 0, 2, 3)
+        .reshape(taps, parts * middle_rows, hidden)
+    )
+    w_last = jnp.concatenate(
         [
-            in_bias[block_number],
-            norm2_gain[block_number],
-            norm2_bias[block_number],
-            conv_bias[block_number],
-            norm3_gain[block_number],
-            norm3_bias[block_number],
-        ]
-    )
-    w_first, w_middle, w_last = (
-        lax.all_gather(w_first, "seq", axis=1, tiled=True),
-        lax.all_gather(w_middle, "seq", axis=2, tiled=True),
-        lax.all_gather(w_last, "seq", axis=1, tiled=True),
-    )
-    w_first, w_middle, w_last, wide_vectors, narrow_vectors = (
-        lax.all_gather(w_first, "dp", axis=0, tiled=True),
-        lax.all_gather(w_middle, "dp", axis=1, tiled=True),
-        lax.all_gather(w_last, "dp", axis=0, tiled=True),
-        lax.all_gather(wide_vectors, "dp", axis=1, tiled=True),
-        lax.all_gather(narrow_vectors, "dp", axis=1, tiled=True),
-    )
-    return (
-        w_first,
-        w_middle,
-        w_last,
-        wide_vectors.astype(jnp.float32),
-        narrow_vectors.astype(jnp.float32),
-    )
+            whole[:, straight + i * middle_rows : straight + (i + 1) * middle_rows].reshape(
+                parts * middle_rows, hidden
+            )
+            for i in range(folds)
+        ],
+        axis=1,
+    )
+    flat = whole[:, straight + folds * middle_rows :].reshape(parts, -1).astype(jnp.float32)
+    wide_end = 3 * first_rows
+    wide = flat[:, :wide_end].reshape(parts, 3, first_rows).transpose(1, 0, 2).reshape(3, -1)
+    narrow = (
+        flat[:, wide_end : wide_end + 6 * middle_rows]
+        .reshape(parts, 6, middle_rows)
+        .transpose(1, 0, 2)
+        .reshape(6, -1)
+    )
+    return (w_first, w_middle, w_last, wide, narrow)
 
 
 def block_forward_pass(inputs, weights, flag_list, dilation_step):
@@ -168,9 +208,8 @@
     return (output, (act_one, projected, tap_rows, conv_out, act_three))
 
 
-def backward_block(inputs, upstream, weights, flag_list, dilation_step):
+def backward_block(inputs, upstream, weights, kept_values, flag_list, dilation_step):
     w_first, w_middle, w_last, wide_vectors, narrow_vectors = weights
-    unused_slot, kept_values = block_forward_pass(inputs, weights, flag_list, dilation_step)
     act_one, projected, tap_rows, conv_out, act_three = kept_values
     row_count, seq_len, model_width = inputs.shape
     hidden = w_middle.shape[1]
@@ -217,26 +256,64 @@
 
 def reduce_grads(block_grads):
     grad_first, grad_middle, grad_last, wide_grads, narrow_grads = block_grads
-    wide_grads, narrow_grads = lax.psum((wide_grads, narrow_grads), "seq")
-    grad_first, grad_middle, grad_last, wide_grads, narrow_grads = (
-        lax.psum_scatter(grad_first, "dp", scatter_dimension=0, tiled=True),
-        lax.psum_scatter(grad_middle, "dp", scatter_dimension=1, tiled=True),
-        lax.psum_scatter(grad_last, "dp", scatter_dimension=0, tiled=True),
-        lax.psum_scatter(wide_grads, "dp", scatter_dimension=1, tiled=True),
-        lax.psum_scatter(narrow_grads, "dp", scatter_dimension=1, tiled=True),
-    )
-    grad_first, grad_middle, grad_last = (
-        lax.psum_scatter(
-            grad_first.astype(jnp.bfloat16), "seq", scatter_dimension=1, tiled=True
-        ).astype(jnp.float32),
-        lax.psum_scatter(
-            grad_middle.astype(jnp.bfloat16), "seq", scatter_dimension=2, tiled=True
-        ).astype(jnp.float32),
-        lax.psum_scatter(
-            grad_last.astype(jnp.bfloat16), "seq", scatter_dimension=1, tiled=True
-        ).astype(jnp.float32),
-    )
-    return (grad_first, grad_middle, grad_last, wide_grads, narrow_grads)
+    parts = lax.axis_size("dp")
+    count = lax.axis_size("seq")
+    me = lax.axis_index("seq")
+    taps, hidden, _ = grad_middle.shape
+    first_rows = grad_first.shape[0] // parts
+    middle_rows = hidden // parts
+    width = hidden // count
+    folds = grad_last.shape[1] // hidden
+    short = jnp.bfloat16
+    vectors = jnp.concatenate(
+        [
+            wide_grads.reshape(3, parts, first_rows).transpose(1, 0, 2).reshape(parts, -1),
+            narrow_grads.reshape(6, parts, middle_rows).transpose(1, 0, 2).reshape(parts, -1),
+        ],
+        axis=1,
+    ).astype(short)
+    length = vectors.shape[1]
+    rows = -(-length // (16 * hidden)) * 16
+    vectors = jnp.pad(vectors, ((0, 0), (0, rows * hidden - length))).reshape(parts, rows, hidden)
+    pieces = [
+        grad_first.astype(short).reshape(parts, first_rows, hidden),
+        grad_middle.astype(short)
+        .reshape(taps, parts, middle_rows, hidden)
+        .transpose(1, 0, 2, 3)
+        .reshape(parts, taps * middle_rows, hidden),
+    ]
+    pieces += [
+        grad_last[:, i * hidden : (i + 1) * hidden].astype(short).reshape(parts, middle_rows, hidden)
+        for i in range(folds)
+    ]
+    mine = lax.psum_scatter(
+        jnp.concatenate(pieces + [vectors], axis=1), "dp", scatter_dimension=0, tiled=False
+    )
+    straight = first_rows + taps * middle_rows
+    total = straight + folds * middle_rows
+    upper = mine[:straight].reshape(straight, count, width).transpose(1, 0, 2)
+    lower = unfolded_columns(mine[straight:total], folds, count)
+    vector_rows = -(-length // width)
+    flat = mine[total:].reshape(-1)[:length]
+    flat = jnp.pad(flat, (0, vector_rows * width - length)).reshape(1, vector_rows, width)
+    ring = jnp.concatenate([upper, lower, jnp.broadcast_to(flat, (count,) + flat.shape[1:])], axis=1)
+    ring = jnp.concatenate([ring, ring])
+    ring = lax.dynamic_slice_in_dim(ring, me, count, axis=0)
+    held = [ring[0]] + [shifted(ring[step], step) for step in range(1, count)]
+    held = [block.astype(jnp.float32) for block in held]
+    while len(held) > 1:
+        half = len(held) // 2
+        held = [held[i] + held[i + half] for i in range(half)]
+    summed = held[0]
+    last = summed[straight:total].reshape(folds, middle_rows, width).transpose(1, 0, 2)
+    flat = summed[total:].reshape(-1)
+    return (
+        summed[:first_rows],
+        summed[first_rows:straight].reshape(taps, middle_rows, width),
+        last.reshape(middle_rows, folds * width),
+        flat[: 3 * first_rows].reshape(3, first_rows),
+        flat[3 * first_rows : length].reshape(6, middle_rows),
+    )
 
 
 def local(
@@ -275,16 +352,19 @@
     early_tap_flags = kernel_tap_flags(protein_lengths, token_positions, FIRST_DILATION)
     later_tap_flags = kernel_tap_flags(protein_lengths, token_positions, SECOND_DILATION)
     hidden_before_blocks = tokens.astype(jnp.float32)
-    hidden_after_first, unused_slot = block_forward_pass(
-        hidden_before_blocks, block_params_list(0, device_shards), early_tap_flags, FIRST_DILATION
-    )
-    hidden_after_second, unused_slot = block_forward_pass(
-        hidden_after_first, block_params_list(1, device_shards), later_tap_flags, SECOND_DILATION
+    early_weights = gathered_params(0, device_shards)
+    late_weights = gathered_params(1, device_shards)
+    hidden_after_first, early_kept = block_forward_pass(
+        hidden_before_blocks, early_weights, early_tap_flags, FIRST_DILATION
+    )
+    hidden_after_second, late_kept = block_forward_pass(
+        hidden_after_first, late_weights, later_tap_flags, SECOND_DILATION
     )
     gradient_after_first, grads_late = backward_block(
         hidden_after_first,
         cotangent.astype(jnp.float32),
-        block_params_list(1, device_shards),
+        late_weights,
+        late_kept,
         later_tap_flags,
         SECOND_DILATION,
     )
@@ -292,7 +372,8 @@
     grad_stream_zero, grads_early = backward_block(
         hidden_before_blocks,
         gradient_after_first,
-        block_params_list(0, device_shards),
+        early_weights,
+        early_kept,
         early_tap_flags,
         FIRST_DILATION,
     )

time: 926 us -> 538 us (0.58)
  waiting for transfers between devices: 452 us -> 229 us
  blocking collectives: 165 us -> 0 us
  local copies, waits for them, and re-layouts: 91.2 us -> 123 us
  matrix products: 80.5 us -> 59.2 us
  other arithmetic: 79.8 us -> 66.5 us
  starting transfers between devices: 24.5 us -> 34.2 us
    unnamed x32 -> x4, waiting for transfers between devices: 255 us -> 0.07 us
    all_gather x10 -> x0, blocking collectives: 153 us -> none  [the longest x2 40.5 us: block_params_list(): lax.all_gather(w_middle, 'seq', axis=2, tiled=True)]
    reduce_scatter x6 -> x2, waiting for transfers between devices: 182 us -> 58.3 us  [reduce_grads(): lax.psum_scatter(jnp.concatenate(pieces + [vectors], axis=1), 'dp', scatt...]
    ppermute x0 -> x12, waiting for transfers between devices: none -> 101 us  [shifted(): lax.ppermute(block, 'seq', [(i, (i + step) % count) for i in range(count)])]
    all_gather x6 -> x2, waiting for transfers between devices: 0.05 us -> 61.8 us  [gathered_params(): whole = lax.all_gather(jnp.concatenate([upper, lower, vectors]), 'dp')]
    slice x8 -> x51, local copies, waits for them, and re-layouts: 1.06 us -> 24.7 us  [the longest x2 5.04 us: gathered_params(): whole[:, first_rows:straight].reshape(parts, taps, middle_rows, hidden)]
    psum x1 -> x0, blocking collectives: 12.1 us -> none  [reduce_grads(): wide_grads, narrow_grads = lax.psum((wide_grads, narrow_grads), 'seq')]
    convert_element_type x2, other arithmetic: 14.1 us -> 2.64 us  [block_forward_pass(): act_one = norm_gelu(inputs.reshape(row_count * seq_len, model_width), wid...]
  transfers between devices with their start and end apart: 30 -> 24, of which waited for: 18 -> 15; matrix products, arithmetic and copies ran while one was open for 25% -> 26% of each run, Pallas kernels for 0% -> 0%
where the time goes in v1:
time: 538 us; the launch traced here: 528 us
  waiting for transfers between devices  229 us (43%)
  local copies, waits for them, and re-layouts  123 us (23%)
  other arithmetic  66.5 us (12%)
  matrix products  59.2 us (11%)
  starting transfers between devices  34.2 us (6%)
  between operations  15.8 us (3%)
    ppermute x12, waiting for transfers between devices, shifted(): lax.ppermute(block, 'seq', [(i, (i + step) % count) for i in range(count)])  101 us
    all_gather x2, waiting for transfers between devices, gathered_params(): whole = lax.all_gather(jnp.concatenate([upper, lower, vectors]), 'dp')  61.8 us
    reduce_scatter x2, waiting for transfers between devices, reduce_grads(): lax.psum_scatter(jnp.concatenate(pieces + [vectors], axis=1), 'dp', scatt...  58.3 us
    unnamed x174, local copies, waits for them, and re-layouts  34.6 us
    unnamed x24, other arithmetic  27.8 us
    dot_general x6, matrix products, contract_rows(): lax.dot_general(left_rows, right_rows, (((0,), (0,)), ((), ())), preferre...  20.6 us
    dot_general x4, matrix products, times_transpose(): lax.dot_general(left_rows, weight, (((1,), (1,)), ((), ())), preferred_el...  16.6 us
    transpose x2, local copies, waits for them, and re-layouts, backward_block(): flipped = jnp.transpose(w_middle, (0, 2, 1)).reshape(KER * hidden, hidden)  15.8 us
  transfers between devices with their start and end apart: 24, of which 15 were waited for; matrix products, arithmetic and copies ran while one was open for 26% of the time, Pallas kernels for 0%

profile of v1, /device:TPU:17, one launch (start us, length us, event | category | flops | bytes accessed | tf_op | source)
XLA Modules:
  0.0 528.0 jit_solution(8533641125456791288)
XLA Ops:
  14.4 5.5 %collective-permute-done = bf16[720,160]{1,0:T(8,128)(2,1)S(1)} collective-permute-done((bf16[720,160]{1,0:T(8,128)(2,1)S(1)}, bf16[720,160]{1,0:T(8,128)(2,1)S(1)}, u32[]{:S(2)}, u32[]{:S(2)}) %collective-permute-start) | collective-permute-done | bytes 230432 | tf_op jit(solution)/shard_map/ppermute | solution.py:99
  19.9 21.6 %collective-permute-done.1 = bf16[720,160]{1,0:T(8,128)(2,1)S(1)} collective-permute-done((bf16[720,160]{1,0:T(8,128)(2,1)S(1)}, bf16[720,160]{1,0:T(8,128)(2,1)S(1)}, u32[]{:S(2)}, u32[]{:S(2)}) %collective-permute-start.1) | collective-permute-done | bytes 230432 | tf_op jit(solution)/shard_map/ppermute | solution.py:99
  52.9 7.0 %collective-permute-done.5 = bf16[720,160]{1,0:T(8,128)(2,1)S(1)} collective-permute-done((bf16[720,160]{1,0:T(8,128)(2,1)S(1)}, bf16[720,160]{1,0:T(8,128)(2,1)S(1)}, u32[]{:S(2)}, u32[]{:S(2)}) %collective-permute-start.5) | collective-permute-done | bytes 230432 | tf_op jit(solution)/shard_map/ppermute | solution.py:99
  59.9 21.8 %collective-permute-done.6 = bf16[720,160]{1,0:T(8,128)(2,1)S(1)} collective-permute-done((bf16[720,160]{1,0:T(8,128)(2,1)S(1)}, bf16[720,160]{1,0:T(8,128)(2,1)S(1)}, u32[]{:S(2)}, u32[]{:S(2)}) %collective-permute-start.6) | collective-permute-done | bytes 230432 | tf_op jit(solution)/shard_map/ppermute | solution.py:99
  90.9 12.0 %all-gather.5.cloned.1.call-done = bf16[5888,640]{1,0:T(8,128)(2,1)} async-done(((bf16[736,640]{1,0:T(8,128)(2,1)}), bf16[5888,640]{1,0:T(8,128)(2,1)}) %all-gather.5.cloned.1.call-update) | async-done | bytes 7536656 | tf_op jit(solution)/shard_map/all_gather | solution.py:159
  106.3 49.8 %all-gather.7.cloned.1.call-done = bf16[5888,640]{1,0:T(8,128)(2,1)} async-done(((bf16[736,640]{1,0:T(8,128)(2,1)}), bf16[5888,640]{1,0:T(8,128)(2,1)}) %all-gather.7.cloned.1.call-update) | async-done | bytes 7536656 | tf_op jit(solution)/shard_map/all_gather | solution.py:159
  210.7 7.9 %copy.232 = bf16[5,640,640]{2,1,0:T(8,128)(2,1)} copy(bf16[5,640,640]{1,2,0:T(8,128)(2,1)} %bitcast.383) | data formatting | bytes 8192000 | tf_op jit(solution)/shard_map/transpose | solution.py:226
  230.5 7.9 %collective-permute-done.9 = bf16[2,256,640]{1,0,2:T(2,128)(2,1)} collective-permute-done((bf16[2,256,640]{1,0,2:T(2,128)(2,1)S(1)}, bf16[2,256,640]{1,0,2:T(2,128)(2,1)}, u32[]{:S(2)}, u32[]{:S(2)}) %collective-permute-start.9) | collective-permute-done | bytes 655392 | tf_op jit(solution)/shard_map/ppermute | solution.py:22
  264.5 4.8 convolution_convert_fusion.4
  285.0 4.3 multiply_reduce_fusion.7
  291.3 4.6 multiply_reduce_fusion
  309.2 8.0 %copy.239 = bf16[5,640,640]{2,1,0:T(8,128)(2,1)} copy(bf16[5,640,640]{1,2,0:T(8,128)(2,1)} %bitcast.379) | data formatting | bytes 8192000 | tf_op jit(solution)/shard_map/transpose | solution.py:226
  317.2 5.2 multiply_reduce_fusion.8
  329.7 4.3 collective-permute-start.13
  334.1 4.6 convolution_convert_fusion.2
  338.7 4.4 convolution_convert_fusion.5
  346.4 4.5 copy.240
  371.0 4.5 multiply_reduce_fusion.2
  399.3 58.3 %reduce-scatter.3.cloned.1.call-done = bf16[1,736,640]{2,1,0:T(8,128)(2,1)} async-done(((bf16[8,736,640]{2,1,0:T(8,128)(2,1)}), bf16[1,736,640]{2,1,0:T(8,128)(2,1)}) %reduce-scatter.3.cloned.1.call-update) | async-done | bytes 942096 | tf_op jit(solution)/shard_map/reduce_scatter | solution.py:289
  460.3 4.3 fusion.57
  470.5 9.7 %collective-permute-done.14 = bf16[726,160]{0,1:T(8,128)(2,1)S(1)} collective-permute-done((bf16[726,160]{0,1:T(8,128)(2,1)S(1)}, bf16[726,160]{0,1:T(8,128)(2,1)S(1)}, u32[]{:S(2)}, u32[]{:S(2)}) %collective-permute-start.14) | collective-permute-done | bytes 232352 | tf_op jit(solution)/shard_map/ppermute | solution.py:99
  480.2 15.4 %collective-permute-done.15 = bf16[726,160]{0,1:T(8,128)(2,1)S(1)} collective-permute-done((bf16[726,160]{0,1:T(8,128)(2,1)S(1)}, bf16[726,160]{0,1:T(8,128)(2,1)S(1)}, u32[]{:S(2)}, u32[]{:S(2)}) %collective-permute-start.15) | collective-permute-done | bytes 232352 | tf_op jit(solution)/shard_map/ppermute | solution.py:99
  496.4 4.9 collective-permute-done.17
  501.3 9.2 %collective-permute-done.18 = bf16[726,160]{0,1:T(8,128)(2,1)S(1)} collective-permute-done((bf16[726,160]{0,1:T(8,128)(2,1)S(1)}, bf16[726,160]{0,1:T(8,128)(2,1)S(1)}, u32[]{:S(2)}, u32[]{:S(2)}) %collective-permute-start.18) | collective-permute-done | bytes 232352 | tf_op jit(solution)/shard_map/ppermute | solution.py:99
  (505 shorter events, 227.6 us)
Async XLA Ops:
  7.3 95.6 %all-gather.5.cloned.1.call-start = ((), (), s32[]{:S(2)}) async-start(), calls=%async_computation.4 | async-start | bytes 8478720 | tf_op jit(solution)/shard_map/all_gather | solution.py:159
  10.4 9.5 %collective-permute-start = (bf16[720,160]{1,0:T(8,128)(2,1)S(1)}, bf16[720,160]{1,0:T(8,128)(2,1)S(1)}, u32[]{:S(2)}, u32[]{:S(2)}) collective-permute-start(bf16[720,160]{1,0:T(8,128)(2,1)S(1)} %pad_maximum_fusion.19), channel_id=1, source_target_pairs={{0,3},{1,0},{2,1},{3,2},{4,7},{5,4},{6,5},{7,6},{8,11},{9,8},{10,9... | collective-permute-start | bytes 691208 | tf_op jit(solution)/shard_map/ppermute | solution.py:99
  10.6 31.0 %collective-permute-start.1 = (bf16[720,160]{1,0:T(8,128)(2,1)S(1)}, bf16[720,160]{1,0:T(8,128)(2,1)S(1)}, u32[]{:S(2)}, u32[]{:S(2)}) collective-permute-start(bf16[720,160]{1,0:T(8,128)(2,1)S(1)} %pad_maximum_fusion.19), channel_id=1, source_target_pairs={{0,2},{1,3},{2,0},{3,1},{4,6},{5,7},{6,4},{7,5},{8,10},{9,11},{10,... | collective-permute-start | bytes 691208 | tf_op jit(solution)/shard_map/ppermute | solution.py:99
  13.8 31.3 %collective-permute-start.2 = (bf16[720,160]{1,0:T(8,128)(2,1)S(1)}, bf16[720,160]{1,0:T(8,128)(2,1)S(1)}, u32[]{:S(2)}, u32[]{:S(2)}) collective-permute-start(bf16[720,160]{1,0:T(8,128)(2,1)S(1)} %pad_maximum_fusion.19), channel_id=1, source_target_pairs={{0,1},{1,2},{2,3},{3,0},{4,5},{5,6},{6,7},{7,4},{8,9},{9,10},{10,1... | collective-permute-start | bytes 691208 | tf_op jit(solution)/shard_map/ppermute | solution.py:99
  50.8 105.3 %all-gather.7.cloned.1.call-start = ((), (), s32[]{:S(2)}) async-start(), calls=%async_computation.5 | async-start | bytes 8478720 | tf_op jit(solution)/shard_map/all_gather | solution.py:159
  51.0 8.9 %collective-permute-start.5 = (bf16[720,160]{1,0:T(8,128)(2,1)S(1)}, bf16[720,160]{1,0:T(8,128)(2,1)S(1)}, u32[]{:S(2)}, u32[]{:S(2)}) collective-permute-start(bf16[720,160]{1,0:T(8,128)(2,1)S(1)} %pad_maximum_fusion.20), channel_id=1, source_target_pairs={{0,3},{1,0},{2,1},{3,2},{4,7},{5,4},{6,5},{7,6},{8,11},{9,8},{10,9... | collective-permute-start | bytes 691208 | tf_op jit(solution)/shard_map/ppermute | solution.py:99
  51.1 30.6 %collective-permute-start.6 = (bf16[720,160]{1,0:T(8,128)(2,1)S(1)}, bf16[720,160]{1,0:T(8,128)(2,1)S(1)}, u32[]{:S(2)}, u32[]{:S(2)}) collective-permute-start(bf16[720,160]{1,0:T(8,128)(2,1)S(1)} %pad_maximum_fusion.20), channel_id=1, source_target_pairs={{0,2},{1,3},{2,0},{3,1},{4,6},{5,7},{6,4},{7,5},{8,10},{9,11},{10,... | collective-permute-start | bytes 691208 | tf_op jit(solution)/shard_map/ppermute | solution.py:99
  51.2 32.4 %collective-permute-start.7 = (bf16[720,160]{1,0:T(8,128)(2,1)S(1)}, bf16[720,160]{1,0:T(8,128)(2,1)S(1)}, u32[]{:S(2)}, u32[]{:S(2)}) collective-permute-start(bf16[720,160]{1,0:T(8,128)(2,1)S(1)} %pad_maximum_fusion.20), channel_id=1, source_target_pairs={{0,1},{1,2},{2,3},{3,0},{4,5},{5,6},{6,7},{7,4},{8,9},{9,10},{10,1... | collective-permute-start | bytes 691208 | tf_op jit(solution)/shard_map/ppermute | solution.py:99
  89.4 307.2 %reduce-scatter.5.cloned.1.call-start = ((), (), s32[]{:S(2)}) async-start(), calls=%async_computation.3 | async-start | bytes 8478720 | tf_op jit(solution)/shard_map/reduce_scatter | solution.py:289
  165.9 14.4 %collective-permute-start.3 = (bf16[2,128,640]{1,0,2:T(2,128)(2,1)S(1)}, bf16[2,128,640]{1,0,2:T(2,128)(2,1)S(1)}, u32[]{:S(2)}, u32[]{:S(2)}) collective-permute-start(bf16[2,128,640]{1,0,2:T(2,128)(2,1)S(1)} %get-tuple-element.161), channel_id=1, source_target_pairs={{0,1},{1,2},{2,3},{4,5},{5,6},{6,7},{8,9},{9,10},{10,11},{12,13},{... | collective-permute-start | bytes 983048 | tf_op jit(solution)/shard_map/ppermute | solution.py:19
  169.9 13.4 %collective-permute-start.4 = (bf16[2,128,640]{1,0,2:T(2,128)(2,1)S(1)}, bf16[2,128,640]{1,0,2:T(2,128)(2,1)S(1)}, u32[]{:S(2)}, u32[]{:S(2)}) collective-permute-start(bf16[2,128,640]{1,0,2:T(2,128)(2,1)S(1)} %get-tuple-element.160), channel_id=1, source_target_pairs={{1,0},{2,1},{3,2},{5,4},{6,5},{7,6},{9,8},{10,9},{11,10},{13,12},{... | collective-permute-start | bytes 983048 | tf_op jit(solution)/shard_map/ppermute | solution.py:22
  202.4 23.9 %collective-permute-start.8 = (bf16[2,256,640]{1,0,2:T(2,128)(2,1)S(1)}, bf16[2,256,640]{1,0,2:T(2,128)(2,1)}, u32[]{:S(2)}, u32[]{:S(2)}) collective-permute-start(bf16[2,256,640]{1,0,2:T(2,128)(2,1)S(1)} %copy.220), channel_id=1, source_target_pairs={{0,1},{1,2},{2,3},{4,5},{5,6},{6,7},{8,9},{9,10},{10,11},{12,13},{... | collective-permute-start | bytes 1966088 | tf_op jit(solution)/shard_map/ppermute | solution.py:19
  221.2 17.1 %collective-permute-start.9 = (bf16[2,256,640]{1,0,2:T(2,128)(2,1)S(1)}, bf16[2,256,640]{1,0,2:T(2,128)(2,1)}, u32[]{:S(2)}, u32[]{:S(2)}) collective-permute-start(bf16[2,256,640]{1,0,2:T(2,128)(2,1)S(1)} %copy.220), channel_id=1, source_target_pairs={{1,0},{2,1},{3,2},{5,4},{6,5},{7,6},{9,8},{10,9},{11,10},{13,12},{... | collective-permute-start | bytes 1966088 | tf_op jit(solution)/shard_map/ppermute | solution.py:22
  254.7 20.1 %collective-permute-start.10 = (bf16[2,256,640]{1,0,2:T(2,128)(2,1)S(1)}, bf16[2,256,640]{1,0,2:T(2,128)(2,1)}, u32[]{:S(2)}, u32[]{:S(2)}) collective-permute-start(bf16[2,256,640]{1,0,2:T(2,128)(2,1)S(1)} %copy.226), channel_id=1, source_target_pairs={{1,0},{2,1},{3,2},{5,4},{6,5},{7,6},{9,8},{10,9},{11,10},{13,12},{... | collective-permute-start | bytes 1966088 | tf_op jit(solution)/shard_map/ppermute | solution.py:22
  256.9 22.1 %collective-permute-start.11 = (bf16[2,256,640]{1,0,2:T(2,128)(2,1)S(1)}, bf16[2,256,640]{1,0,2:T(2,128)(2,1)}, u32[]{:S(2)}, u32[]{:S(2)}) collective-permute-start(bf16[2,256,640]{1,0,2:T(2,128)(2,1)S(1)} %copy.226), channel_id=1, source_target_pairs={{0,1},{1,2},{2,3},{4,5},{5,6},{6,7},{8,9},{9,10},{10,11},{12,13},{... | collective-permute-start | bytes 1966088 | tf_op jit(solution)/shard_map/ppermute | solution.py:19
  309.1 148.5 %reduce-scatter.3.cloned.1.call-start = ((), (), s32[]{:S(2)}) async-start(), calls=%async_computation.2 | async-start | bytes 8478720 | tf_op jit(solution)/shard_map/reduce_scatter | solution.py:289
  327.8 24.5 %collective-permute-start.12 = (bf16[2,128,640]{1,0,2:T(2,128)(2,1)}, bf16[2,128,640]{1,0,2:T(2,128)(2,1)}, u32[]{:S(2)}, u32[]{:S(2)}) collective-permute-start(bf16[2,128,640]{1,0,2:T(2,128)(2,1)} %get-tuple-element.159), channel_id=1, source_target_pairs={{1,0},{2,1},{3,2},{5,4},{6,5},{7,6},{9,8},{10,9},{11,10},{13,12},{... | collective-permute-start | bytes 983048 | tf_op jit(solution)/shard_map/ppermute | solution.py:22
  329.7 28.0 %collective-permute-start.13 = (bf16[2,128,640]{1,0,2:T(2,128)(2,1)}, bf16[2,128,640]{1,0,2:T(2,128)(2,1)}, u32[]{:S(2)}, u32[]{:S(2)}) collective-permute-start(bf16[2,128,640]{1,0,2:T(2,128)(2,1)} %get-tuple-element.158), channel_id=1, source_target_pairs={{0,1},{1,2},{2,3},{4,5},{5,6},{6,7},{8,9},{9,10},{10,11},{12,13},{... | collective-permute-start | bytes 983048 | tf_op jit(solution)/shard_map/ppermute | solution.py:19
  464.7 15.5 %collective-permute-start.14 = (bf16[726,160]{0,1:T(8,128)(2,1)S(1)}, bf16[726,160]{0,1:T(8,128)(2,1)S(1)}, u32[]{:S(2)}, u32[]{:S(2)}) collective-permute-start(bf16[726,160]{0,1:T(8,128)(2,1)S(1)} %get-tuple-element.152), channel_id=1, source_target_pairs={{0,2},{1,3},{2,0},{3,1},{4,6},{5,7},{6,4},{7,5},{8,10},{9,11},{10,... | collective-permute-start | bytes 696968 | tf_op jit(solution)/shard_map/ppermute | solution.py:99
  465.0 30.7 %collective-permute-start.15 = (bf16[726,160]{0,1:T(8,128)(2,1)S(1)}, bf16[726,160]{0,1:T(8,128)(2,1)S(1)}, u32[]{:S(2)}, u32[]{:S(2)}) collective-permute-start(bf16[726,160]{0,1:T(8,128)(2,1)S(1)} %get-tuple-element.153), channel_id=1, source_target_pairs={{0,1},{1,2},{2,3},{3,0},{4,5},{5,6},{6,7},{7,4},{8,9},{9,10},{10,1... | collective-permute-start | bytes 696968 | tf_op jit(solution)/shard_map/ppermute | solution.py:99
  466.3 29.7 %collective-permute-start.16 = (bf16[726,160]{0,1:T(8,128)(2,1)S(1)}, bf16[726,160]{0,1:T(8,128)(2,1)S(1)}, u32[]{:S(2)}, u32[]{:S(2)}) collective-permute-start(bf16[726,160]{0,1:T(8,128)(2,1)S(1)} %get-tuple-element.154), channel_id=1, source_target_pairs={{0,3},{1,0},{2,1},{3,2},{4,7},{5,4},{6,5},{7,6},{8,11},{9,8},{10,9... | collective-permute-start | bytes 696968 | tf_op jit(solution)/shard_map/ppermute | solution.py:99
  467.3 34.0 %collective-permute-start.17 = (bf16[726,160]{0,1:T(8,128)(2,1)S(1)}, bf16[726,160]{0,1:T(8,128)(2,1)S(1)}, u32[]{:S(2)}, u32[]{:S(2)}) collective-permute-start(bf16[726,160]{0,1:T(8,128)(2,1)S(1)} %get-tuple-element.155), channel_id=1, source_target_pairs={{0,2},{1,3},{2,0},{3,1},{4,6},{5,7},{6,4},{7,5},{8,10},{9,11},{10,... | collective-permute-start | bytes 696968 | tf_op jit(solution)/shard_map/ppermute | solution.py:99
  470.5 39.9 %collective-permute-start.18 = (bf16[726,160]{0,1:T(8,128)(2,1)S(1)}, bf16[726,160]{0,1:T(8,128)(2,1)S(1)}, u32[]{:S(2)}, u32[]{:S(2)}) collective-permute-start(bf16[726,160]{0,1:T(8,128)(2,1)S(1)} %get-tuple-element.156), channel_id=1, source_target_pairs={{0,1},{1,2},{2,3},{3,0},{4,5},{5,6},{6,7},{7,4},{8,9},{9,10},{10,1... | collective-permute-start | bytes 696968 | tf_op jit(solution)/shard_map/ppermute | solution.py:99
  480.2 30.2 %collective-permute-start.19 = (bf16[726,160]{0,1:T(8,128)(2,1)S(1)}, bf16[726,160]{0,1:T(8,128)(2,1)S(1)}, u32[]{:S(2)}, u32[]{:S(2)}) collective-permute-start(bf16[726,160]{0,1:T(8,128)(2,1)S(1)} %get-tuple-element.157), channel_id=1, source_target_pairs={{0,3},{1,0},{2,1},{3,2},{4,7},{5,4},{6,5},{7,6},{8,11},{9,8},{10,9... | collective-permute-start | bytes 696968 | tf_op jit(solution)/shard_map/ppermute | solution.py:99
  (72 other events, 396.1 us)
Sparse Core Ops, SparseCore 0:
  51.0 51.8 all-gather.4
  105.3 50.7 all-gather.6
  309.2 68.8 reduce-scatter.4
  387.5 70.0 reduce-scatter.2

commit v2 on v1

v2 whole, which is shorter than its diff:
```python
import functools
import math

import jax
import jax.numpy as jnp
from jax import lax
from jax.experimental import pallas as pl
from jax.experimental.pallas import tpu as pltpu
from jax.sharding import PartitionSpec as P

KER = 5
FIRST_DILATION = 64
SECOND_DILATION = 128


epsilon = 1e-05
CUBIC = 0.044715
SLOPE = math.sqrt(2.0 / math.pi)
VECTOR_ROWS = 16


def seq_neighbours(block, width):
    count = lax.axis_size("seq")
    forward = [(i, i + 1) for i in range(count - 1)]
    backward = [(target, source) for source, target in forward]
    low = lax.ppermute(block[:, block.shape[1] - width :], "seq", forward)
    high = lax.ppermute(block[:, :width], "seq", backward)
    return low, high


def normalized(values):
    centred = values - jnp.mean(values, -1, keepdims=True)
    scale = lax.rsqrt(jnp.mean(centred * centred, -1, keepdims=True) + epsilon)
    return centred * scale, scale


def gelu(h):
    return 0.5 * h * (1.0 + jnp.tanh(SLOPE * (h + CUBIC * (h * h * h))))


def norm_gelu(values, gain_vector, bias_vector):
    return gelu(normalized(values)[0] * gain_vector + bias_vector)


def norm_gelu_back(incoming, values, gain_vector, bias_vector):
    n, scale = normalized(values)
    h = n * gain_vector + bias_vector
    square = h * h
    t = jnp.tanh(SLOPE * (h + CUBIC * (square * h)))
    slope = 0.5 * (1.0 + t) + (0.5 * SLOPE) * h * (1.0 - t * t) * (1.0 + (3.0 * CUBIC) * square)
    dh = incoming * slope
    dn = dh * gain_vector
    back = dn - jnp.mean(dn, -1, keepdims=True) - n * jnp.mean(dn * n, -1, keepdims=True)
    return back * scale, column_sum(dh * n), column_sum(dh)


def column_sum(values):
    return jnp.sum(values, axis=0, keepdims=True)


def matmul(left, right):
    return jnp.dot(left, right, preferred_element_type=jnp.float32)


def matmul_back(left, right):
    return lax.dot_general(
        left, right, (((1,), (1,)), ((), ())), preferred_element_type=jnp.float32
    )


def matmul_rows(left, right):
    return lax.dot_general(
        left, right, (((0,), (0,)), ((), ())), preferred_element_type=jnp.float32
    )


def merged(ref):
    parts, rows, columns = ref.shape
    return ref[...].reshape(parts * rows, columns)


def kernel_tap_flags(lengths, token_positions, dilation_step):
    doc_ends = jnp.cumsum(lengths, axis=1)
    row_total = doc_ends[:, -1:]
    where_pos = token_positions[None, :, None]
    finished = doc_ends[:, None, :] <= where_pos
    doc_start = jnp.sum(jnp.where(finished, lengths[:, None, :], 0), axis=2)
    doc_stop = jnp.min(jnp.where(finished, row_total[:, :, None] + 1, doc_ends[:, None, :]), axis=2)
    is_live = token_positions[None, :] < row_total
    flag_list = []
    for tap_index in range(KER):
        target = token_positions[None, :] + (tap_index - KER // 2) * dilation_step
        flag_list.append(is_live & (target >= doc_start) & (target < doc_stop))
    flag_list += [flag_list[-1]] * (8 - KER)
    return jnp.stack(flag_list, axis=2).astype(jnp.bfloat16)


def project_kernel(x_ref, w_ref, wide_ref, narrow_ref, act_one_ref, u_ref, act_two_ref):
    act_one = norm_gelu(
        x_ref[...].astype(jnp.float32), wide_ref[0:1, :], wide_ref[1:2, :]
    ).astype(jnp.bfloat16)
    act_one_ref[...] = act_one
    u = matmul(act_one, merged(w_ref)) + narrow_ref[0:1, :]
    u_ref[...] = u
    act_two_ref[...] = norm_gelu(u, narrow_ref[1:2, :], narrow_ref[2:3, :]).astype(jnp.bfloat16)


def tap_slices(low_ref, own_ref, high_ref, flag_ref, dilation_step):
    length = own_ref.shape[1]
    width = low_ref.shape[1]
    padded = jnp.concatenate([low_ref[0], own_ref[0], high_ref[0]], axis=0)
    for k in range(KER):
        start = width + (k - KER // 2) * dilation_step
        yield k, padded[start : start + length] * flag_ref[0][:, k : k + 1]


def convolve_kernel(
    dilation_step,
    low_ref,
    own_ref,
    high_ref,
    flag_ref,
    x_ref,
    k0_ref,
    k1_ref,
    k2_ref,
    k3_ref,
    k4_ref,
    left_ref,
    right_ref,
    wide_ref,
    narrow_ref,
    tap_ref,
    v_ref,
    act_three_ref,
    next_ref,
):
    taps = (k0_ref, k1_ref, k2_ref, k3_ref, k4_ref)
    hidden = own_ref.shape[2]
    total = narrow_ref[3:4, :]
    for k, piece in tap_slices(low_ref, own_ref, high_ref, flag_ref, dilation_step):
        tap_ref[:, k * hidden : (k + 1) * hidden] = piece
        total = total + matmul(piece, merged(taps[k]))
    v_ref[...] = total
    act_three = norm_gelu(total, narrow_ref[4:5, :], narrow_ref[5:6, :]).astype(jnp.bfloat16)
    act_three_ref[...] = act_three
    for i, half_ref in enumerate((left_ref, right_ref)):
        columns = slice(i * hidden, (i + 1) * hidden)
        branch = matmul(act_three, merged(half_ref)) + wide_ref[2:3, columns]
        next_ref[:, columns] = (x_ref[:, columns].astype(jnp.float32) + branch).astype(
            next_ref.dtype
        )


def out_back_kernel(
    g_ref, v_ref, left_ref, right_ref, narrow_ref, short_ref, gv_ref, narrow_sum_ref, wide_sum_ref
):
    hidden = v_ref.shape[1]

    @pl.when(pl.program_id(0) == 0)
    def _():
        narrow_sum_ref[...] = jnp.zeros_like(narrow_sum_ref)
        wide_sum_ref[...] = jnp.zeros_like(wide_sum_ref)

    short = g_ref[...].astype(jnp.bfloat16)
    short_ref[...] = short
    wide_sum_ref[0:1, :] += column_sum(short.astype(jnp.float32))
    incoming = matmul_back(short[:, :hidden], merged(left_ref))
    incoming = incoming + matmul_back(short[:, hidden:], merged(right_ref))
    gv, gain_sum, bias_sum = norm_gelu_back(
        incoming, v_ref[...], narrow_ref[4:5, :], narrow_ref[5:6, :]
    )
    gv = gv.astype(jnp.bfloat16)
    gv_ref[...] = gv
    narrow_sum_ref[0:1, :] += column_sum(gv.astype(jnp.float32))
    narrow_sum_ref[1:2, :] += gain_sum
    narrow_sum_ref[2:3, :] += bias_sum


def weight_grad_kernel(tap_ref, gv_ref, act_three_ref, short_ref, pack_ref):
    step = pl.program_id(0)

    def store(value):
        pack_ref[...] = value.astype(jnp.bfloat16).reshape(pack_ref.shape)

    @pl.when(step < KER)
    def _():
        store(matmul_rows(tap_ref[...], gv_ref[...]))

    @pl.when(step >= KER)
    def _():
        store(matmul_rows(act_three_ref[...], short_ref[...]))


def conv_back_kernel(
    dilation_step,
    low_ref,
    own_ref,
    high_ref,
    flag_ref,
    u_ref,
    x_ref,
    g_ref,
    k0_ref,
    k1_ref,
    k2_ref,
    k3_ref,
    k4_ref,
    w_ref,
    wide_ref,
    narrow_ref,
    gu_ref,
    next_ref,
    narrow_sum_ref,
    wide_sum_ref,
):
    @pl.when(pl.program_id(0) == 0)
    def _():
        narrow_sum_ref[...] = jnp.zeros_like(narrow_sum_ref)
        wide_sum_ref[...] = jnp.zeros_like(wide_sum_ref)

    taps = (k0_ref, k1_ref, k2_ref, k3_ref, k4_ref)
    total = None
    for k, piece in tap_slices(low_ref, own_ref, high_ref, flag_ref, dilation_step):
        term = matmul_back(piece, merged(taps[KER - 1 - k]))
        total = term if total is None else total + term
    gu, gain_sum, bias_sum = norm_gelu_back(
        total, u_ref[...], narrow_ref[1:2, :], narrow_ref[2:3, :]
    )
    gu = gu.astype(jnp.bfloat16)
    gu_ref[...] = gu
    narrow_sum_ref[0:1, :] += column_sum(gu.astype(jnp.float32))
    narrow_sum_ref[1:2, :] += gain_sum
    narrow_sum_ref[2:3, :] += bias_sum
    gx, gain_sum, bias_sum = norm_gelu_back(
        matmul_back(gu, merged(w_ref)),
        x_ref[...].astype(jnp.float32),
        wide_ref[0:1, :],
        wide_ref[1:2, :],
    )
    next_ref[...] = g_ref[...].astype(jnp.float32) + gx
    wide_sum_ref[0:1, :] += gain_sum
    wide_sum_ref[1:2, :] += bias_sum


def in_grad_kernel(pack_in_ref, act_one_ref, gu_ref, pack_ref):
    value = matmul_rows(act_one_ref[...], gu_ref[...])
    pack_ref[...] = value.astype(jnp.bfloat16).reshape(pack_ref.shape)


def tiled(rows, columns):
    return pl.BlockSpec((rows, columns), lambda i: (i, 0))


def fixed(*shape):
    return pl.BlockSpec(shape, lambda i: (0,) * len(shape))


def row_block(shape):
    return pl.BlockSpec((1,) + shape[1:], lambda i: (i, 0, 0))


def pack_block(parts, rows, columns, index):
    return pl.BlockSpec((parts, rows, columns), lambda i: (0, index, 0))


def cost(flops, width):
    return pl.CostEstimate(flops=flops, bytes_accessed=width, transcendentals=0)


def call(kernel, grid, in_specs, out_specs, out_shape, flops, moved, name, aliases=None):
    return pl.pallas_call(
        kernel,
        grid=(grid,),
        in_specs=in_specs,
        out_specs=out_specs,
        out_shape=out_shape,
        input_output_aliases=aliases or {},
        cost_estimate=cost(flops, moved),
        compiler_params=pltpu.CompilerParams(vmem_limit_bytes=48 * 1024 * 1024),
        name=name,
    )


def shape_of(shape, dtype):
    return jax.ShapeDtypeStruct(shape, dtype)


class Sizes:
    def __init__(self, pack, model, hidden):
        self.parts = pack.shape[0]
        self.model, self.hidden = model, hidden
        self.first_rows = model // self.parts
        self.middle_rows = hidden // self.parts
        self.folds = model // hidden
        self.conv_at = self.first_rows // self.middle_rows
        self.out_at = self.conv_at + KER

    def first(self):
        return pack_block(self.parts, self.first_rows, self.hidden, 0)

    def taps(self):
        return [
            pack_block(self.parts, self.middle_rows, self.hidden, self.conv_at + k)
            for k in range(KER)
        ]

    def last(self):
        return [
            pack_block(self.parts, self.middle_rows, self.hidden, self.out_at + i)
            for i in range(self.folds)
        ]


def project(inputs, weights):
    pack, wide, narrow = weights
    tokens, model = inputs.shape
    hidden = narrow.shape[1]
    sizes = Sizes(pack, model, hidden)
    tile = min(128, tokens)
    return call(
        project_kernel,
        tokens // tile,
        [tiled(tile, model), sizes.first(), fixed(3, model), fixed(6, hidden)],
        [tiled(tile, model), tiled(tile, hidden), tiled(tile, hidden)],
        [
            shape_of((tokens, model), jnp.bfloat16),
            shape_of((tokens, hidden), jnp.float32),
            shape_of((tokens, hidden), jnp.bfloat16),
        ],
        4 * tokens * model * hidden,
        12 * tokens * model,
        "project",
    )(inputs, pack, wide, narrow)


def convolve(act_two, flags, inputs, weights, dilation_step, next_dtype):
    pack, wide, narrow = weights
    rows, length, hidden = act_two.shape
    tokens, model = inputs.shape
    sizes = Sizes(pack, model, hidden)
    low, high = seq_neighbours(act_two, KER // 2 * dilation_step)
    return call(
        functools.partial(convolve_kernel, dilation_step),
        rows,
        [
            row_block(low.shape),
            row_block(act_two.shape),
            row_block(high.shape),
            row_block(flags.shape),
            tiled(length, model),
            *sizes.taps(),
            *sizes.last(),
            fixed(3, model),
            fixed(6, hidden),
        ],
        [
            tiled(length, KER * hidden),
            tiled(length, hidden),
            tiled(length, hidden),
            tiled(length, model),
        ],
        [
            shape_of((tokens, KER * hidden), jnp.bfloat16),
            shape_of((tokens, hidden), jnp.float32),
            shape_of((tokens, hidden), jnp.bfloat16),
            shape_of((tokens, model), next_dtype),
        ],
        2 * tokens * hidden * (KER * hidden + model),
        16 * tokens * model,
        "convolve",
    )(low, act_two, high, flags, inputs, *([pack] * (KER + 2)), wide, narrow)


def out_back(upstream, conv_out, weights):
    pack, wide, narrow = weights
    tokens, model = upstream.shape
    hidden = narrow.shape[1]
    sizes = Sizes(pack, model, hidden)
    tile = min(128, tokens)
    return call(
        out_back_kernel,
        tokens // tile,
        [tiled(tile, model), tiled(tile, hidden), *sizes.last(), fixed(6, hidden)],
        [tiled(tile, model), tiled(tile, hidden), fixed(8, hidden), fixed(8, model)],
        [
            shape_of((tokens, model), jnp.bfloat16),
            shape_of((tokens, hidden), jnp.bfloat16),
            shape_of((8, hidden), jnp.float32),
            shape_of((8, model), jnp.float32),
        ],
        4 * tokens * model * hidden,
        10 * tokens * model,
        "out_back",
    )(upstream, conv_out, pack, pack, narrow)


def weight_grads(tap_rows, gv, act_three, short, pack):
    tokens, hidden = gv.shape
    model = short.shape[1]
    sizes = Sizes(pack, model, hidden)
    whole = pl.BlockSpec((tokens, hidden), lambda s: (0, 0))
    return call(
        weight_grad_kernel,
        KER + sizes.folds,
        [
            pl.BlockSpec((tokens, hidden), lambda s: (0, jnp.minimum(s, KER - 1))),
            whole,
            whole,
            pl.BlockSpec((tokens, hidden), lambda s: (0, jnp.maximum(s - KER, 0))),
        ],
        pl.BlockSpec(
            (sizes.parts, sizes.middle_rows, hidden), lambda s: (0, sizes.conv_at + s, 0)
        ),
        shape_of(pack.shape, jnp.bfloat16),
        2 * tokens * hidden * (KER * hidden + model),
        8 * tokens * model,
        "weight_grads",
    )(tap_rows, gv, act_three, short)


def conv_back(gv, flags, u, inputs, upstream, weights, dilation_step):
    pack, wide, narrow = weights
    rows, length, hidden = gv.shape
    tokens, model = inputs.shape
    sizes = Sizes(pack, model, hidden)
    low, high = seq_neighbours(gv, KER // 2 * dilation_step)
    return call(
        functools.partial(conv_back_kernel, dilation_step),
        rows,
        [
            row_block(low.shape),
            row_block(gv.shape),
            row_block(high.shape),
            row_block(flags.shape),
            tiled(length, hidden),
            tiled(length, model),
            tiled(length, model),
            *sizes.taps(),
            sizes.first(),
            fixed(3, model),
            fixed(6, hidden),
        ],
        [tiled(length, hidden), tiled(length, model), fixed(8, hidden), fixed(8, model)],
        [
            shape_of((tokens, hidden), jnp.bfloat16),
            shape_of((tokens, model), jnp.float32),
            shape_of((8, hidden), jnp.float32),
            shape_of((8, model), jnp.float32),
        ],
        2 * tokens * hidden * (KER * hidden + model),
        16 * tokens * model,
        "conv_back",
    )(low, gv, high, flags, u, inputs, upstream, *([pack] * (KER + 1)), wide, narrow)


def in_grads(grad_pack, act_one, gu):
    tokens, model = act_one.shape
    hidden = gu.shape[1]
    sizes = Sizes(grad_pack, model, hidden)
    return call(
        in_grad_kernel,
        1,
        [pl.BlockSpec(memory_space=pl.ANY), fixed(tokens, model), fixed(tokens, hidden)],
        sizes.first(),
        shape_of(grad_pack.shape, jnp.bfloat16),
        2 * tokens * hidden * model,
        4 * tokens * model,
        "in_grads",
        {0: 0},
    )(grad_pack, act_one, gu)


def shifted(block, step):
    count = lax.axis_size("seq")
    return lax.ppermute(block, "seq", [(i, (i + step) % count) for i in range(count)])


def weight_pack(block_number, device_shards):
    w_in, w_conv, w_out = (device_shards[i][block_number] for i in (2, 6, 10))
    width = w_in.shape[1]
    folds = w_out.shape[1] // width
    pieces = [w_in, w_conv.reshape(-1, width)]
    pieces += [w_out[:, i * width : (i + 1) * width] for i in range(folds)]
    return jnp.concatenate(pieces, axis=0)


def vector_pack(block_number, device_shards, width):
    order = (0, 1, 11, 3, 4, 5, 7, 8, 9)
    rows = [device_shards[i][block_number] for i in order]
    rows = [jnp.pad(row, (0, width - row.shape[0])) for row in rows]
    return jnp.pad(jnp.stack(rows), ((0, VECTOR_ROWS - len(rows)), (0, 0)))


def seq_gathered(packed):
    count = lax.axis_size("seq")
    me = lax.axis_index("seq")
    held = [packed] + [shifted(packed, step) for step in range(1, count)]
    ring = jnp.stack(held[::-1] + held[::-1])
    return lax.dynamic_slice_in_dim(ring, (count - 1 - me) % count, count, axis=0)


def folded_columns(out_parts):
    count, folds, depth, width = out_parts.shape
    per_fold = count // folds
    return (
        out_parts.reshape(folds, per_fold, folds, depth, width)
        .transpose(0, 3, 1, 2, 4)
        .reshape(folds * depth, per_fold * folds * width)
    )


def unfolded_columns(out_rows, folds, count):
    per_fold = count // folds
    depth = out_rows.shape[0] // folds
    width = out_rows.shape[1] // count
    return (
        out_rows.reshape(folds, depth, per_fold, folds, width)
        .transpose(0, 2, 3, 1, 4)
        .reshape(count, folds * depth, width)
    )


def pack_is_aligned(middle_rows):
    return middle_rows % 16 == 0


def gathered_params(block_number, device_shards):
    w_in, w_conv, w_out = (device_shards[i][block_number] for i in (2, 6, 10))
    first_rows = w_in.shape[0]
    taps, middle_rows, width = w_conv.shape
    folds = w_out.shape[1] // width
    count = lax.axis_size("seq")
    hidden = width * count
    by_seq = seq_gathered(weight_pack(block_number, device_shards))
    straight = first_rows + taps * middle_rows
    total = straight + folds * middle_rows
    upper = by_seq[:, :straight].transpose(1, 0, 2).reshape(straight, hidden)
    lower = folded_columns(by_seq[:, straight:].reshape(count, folds, middle_rows, width))
    vectors = vector_pack(block_number, device_shards, hidden)
    whole = lax.all_gather(jnp.concatenate([upper, lower, vectors]), "dp")
    tail = whole[:, total:].astype(jnp.float32)
    wide = tail[:, :3, :first_rows].transpose(1, 0, 2).reshape(3, -1)
    narrow = tail[:, 3:9, :middle_rows].transpose(1, 0, 2).reshape(6, -1)
    if not pack_is_aligned(middle_rows):
        bounds = [0, first_rows]
        bounds += [first_rows + (k + 1) * middle_rows for k in range(taps + folds)]
        whole = jnp.concatenate(
            [whole[:, a:b].reshape(1, -1, hidden) for a, b in zip(bounds, bounds[1:])], axis=1
        )
    return (whole, wide, narrow)


def reduce_grads(grad_pack, wide_grads, narrow_grads):
    parts = lax.axis_size("dp")
    count = lax.axis_size("seq")
    me = lax.axis_index("seq")
    hidden = narrow_grads.shape[1]
    model = wide_grads.shape[1]
    first_rows = model // parts
    middle_rows = hidden // parts
    width = hidden // count
    folds = model // hidden
    straight = first_rows + KER * middle_rows
    total = straight + folds * middle_rows
    if not pack_is_aligned(middle_rows):
        bounds = [0, model] + [model + (k + 1) * hidden for k in range(KER + folds)]
        grad_pack = jnp.concatenate(
            [grad_pack[0, a:b].reshape(parts, -1, hidden) for a, b in zip(bounds, bounds[1:])]
            + [jnp.zeros((parts, VECTOR_ROWS, hidden), jnp.bfloat16)],
            axis=1,
        )
    vectors = jnp.concatenate(
        [
            jnp.pad(
                block.reshape(-1, parts, rows).transpose(1, 0, 2),
                ((0, 0), (0, 0), (0, hidden - rows)),
            )
            for block, rows in ((wide_grads, first_rows), (narrow_grads, middle_rows))
        ]
        + [jnp.zeros((parts, VECTOR_ROWS - 9, hidden), jnp.float32)],
        axis=1,
    ).astype(jnp.bfloat16)
    grad_pack = lax.dynamic_update_slice(grad_pack, vectors, (0, total, 0))
    mine = lax.psum_scatter(grad_pack, "dp", scatter_dimension=0, tiled=False)
    upper = mine[:straight].reshape(straight, count, width).transpose(1, 0, 2)
    lower = unfolded_columns(mine[straight:total], folds, count)
    fold = -(-first_rows // width)
    tail = mine[total:, : fold * width].reshape(1, VECTOR_ROWS * fold, width)
    tail = jnp.broadcast_to(tail, (count,) + tail.shape[1:])
    ring = jnp.concatenate([upper, lower, tail], axis=1)
    ring = jnp.concatenate([ring, ring])
    ring = lax.dynamic_slice_in_dim(ring, me, count, axis=0)
    held = [ring[0]] + [shifted(ring[step], step) for step in range(1, count)]
    held = [block.astype(jnp.float32) for block in held]
    while len(held) > 1:
        half = len(held) // 2
        held = [held[i] + held[i + half] for i in range(half)]
    summed = held[0]
    last = summed[straight:total].reshape(folds, middle_rows, width).transpose(1, 0, 2)
    tail = summed[total:].reshape(VECTOR_ROWS, fold * width)
    return (
        summed[:first_rows],
        summed[first_rows:straight].reshape(KER, middle_rows, width),
        last.reshape(middle_rows, folds * width),
        tail[:3, :first_rows],
        tail[3:9, :middle_rows],
    )


def block_forward(inputs, weights, flags, dilation_step, next_dtype):
    rows, length, _ = flags.shape
    act_one, u, act_two = project(inputs, weights)
    tap_rows, conv_out, act_three, output = convolve(
        act_two.reshape(rows, length, -1), flags, inputs, weights, dilation_step, next_dtype
    )
    return output, (act_one, u, tap_rows, conv_out, act_three)


def block_backward(inputs, upstream, weights, kept, flags, dilation_step):
    act_one, u, tap_rows, conv_out, act_three = kept
    rows, length, _ = flags.shape
    short, gv, narrow_a, wide_a = out_back(upstream, conv_out, weights)
    pack = weights[0]
    grad_shape = shape_of(
        (pack.shape[0], sum(pack_rows(pack, inputs.shape[1], gv.shape[1])), gv.shape[1]),
        jnp.bfloat16,
    )
    grad_pack = weight_grads(tap_rows, gv, act_three, short, grad_shape)
    gu, result, narrow_b, wide_b = conv_back(
        gv.reshape(rows, length, -1), flags, u, inputs, upstream, weights, dilation_step
    )
    grad_pack = in_grads(grad_pack, act_one, gu)
    wide = jnp.concatenate([wide_b[0:2], wide_a[0:1]])
    narrow = jnp.concatenate([narrow_b[0:3], narrow_a[0:3]])
    return result, (grad_pack, wide, narrow)


def pack_rows(pack, model, hidden):
    parts = pack.shape[0]
    extra = VECTOR_ROWS if pack_is_aligned(hidden // lax.axis_size("dp")) else 0
    return model // parts, (KER * hidden + model) // parts, extra


def local(
    tokens,
    protein_lengths,
    norm1_gain,
    norm1_bias,
    w_in,
    in_bias,
    norm2_gain,
    norm2_bias,
    w_conv,
    conv_bias,
    norm3_gain,
    norm3_bias,
    w_out,
    out_bias,
    cotangent,
):
    device_shards = (
        norm1_gain,
        norm1_bias,
        w_in,
        in_bias,
        norm2_gain,
        norm2_bias,
        w_conv,
        conv_bias,
        norm3_gain,
        norm3_bias,
        w_out,
        out_bias,
    )
    rows, seq_len, model = tokens.shape
    token_positions = lax.axis_index("seq") * seq_len + jnp.arange(seq_len, dtype=jnp.int32)
    early_flags = kernel_tap_flags(protein_lengths, token_positions, FIRST_DILATION)
    later_flags = kernel_tap_flags(protein_lengths, token_positions, SECOND_DILATION)
    early_weights = gathered_params(0, device_shards)
    late_weights = gathered_params(1, device_shards)
    flat_tokens = tokens.reshape(rows * seq_len, model)
    middle, early_kept = block_forward(
        flat_tokens, early_weights, early_flags, FIRST_DILATION, jnp.float32
    )
    middle, late_weights = lax.optimization_barrier((middle, late_weights))
    output, late_kept = block_forward(
        middle, late_weights, later_flags, SECOND_DILATION, jnp.bfloat16
    )
    middle_grad, grads_late = block_backward(
        middle,
        cotangent.reshape(rows * seq_len, model),
        late_weights,
        late_kept,
        later_flags,
        SECOND_DILATION,
    )
    reduced_late = reduce_grads(*grads_late)
    input_grad, grads_early = block_backward(
        flat_tokens, middle_grad, early_weights, early_kept, early_flags, FIRST_DILATION
    )
    reduced_early = reduce_grads(*grads_early)
    first_early, middle_early, last_early, wide_early, narrow_early = reduced_early
    first_late, middle_late, last_late, wide_late, narrow_late = reduced_late
    return (
        output.reshape(tokens.shape),
        input_grad.reshape(tokens.shape),
        jnp.stack([wide_early[0], wide_late[0]]),
        jnp.stack([wide_early[1], wide_late[1]]),
        jnp.stack([first_early, first_late]),
        jnp.stack([narrow_early[0], narrow_late[0]]),
        jnp.stack([narrow_early[1], narrow_late[1]]),
        jnp.stack([narrow_early[2], narrow_late[2]]),
        jnp.stack([middle_early, middle_late]),
        jnp.stack([narrow_early[3], narrow_late[3]]),
        jnp.stack([narrow_early[4], narrow_late[4]]),
        jnp.stack([narrow_early[5], narrow_late[5]]),
        jnp.stack([last_early, last_late]),
        jnp.stack([wide_early[2], wide_late[2]]),
    )


def solution(mesh):
    placed = (
        P("dp", "seq", None),
        P("dp", None),
        P(None, "dp"),
        P(None, "dp"),
        P(None, "dp", "seq"),
        P(None, "dp"),
        P(None, "dp"),
        P(None, "dp"),
        P(None, None, "dp", "seq"),
        P(None, "dp"),
        P(None, "dp"),
        P(None, "dp"),
        P(None, "dp", "seq"),
        P(None, "dp"),
        P("dp", "seq", None),
    )
    return jax.shard_map(
        local,
        mesh=mesh,
        in_specs=placed,
        out_specs=(
            P("dp", "seq", None),
            P("dp", "seq", None),
            P(None, "dp"),
            P(None, "dp"),
            P(None, "dp", "seq"),
            P(None, "dp"),
            P(None, "dp"),
            P(None, "dp"),
            P(None, None, "dp", "seq"),
            P(None, "dp"),
            P(None, "dp"),
            P(None, "dp"),
            P(None, "dp", "seq"),
            P(None, "dp"),
        ),
        check_vma=False,
    )
```

time: 538 us -> 524 us (0.974)
  waiting for transfers between devices: 229 us -> 313 us
  Pallas kernels: 0 us -> 83.3 us
  local copies, waits for them, and re-layouts: 123 us -> 50.7 us
  matrix products: 59.2 us -> 0 us
  other arithmetic: 66.5 us -> 17.9 us
    pallas_call x0 -> x12, Pallas kernels: none -> 83.3 us  [the longest x2 24.6 us: conv_back(): call(functools.partial(conv_back_kernel, dilation_step), rows, [row_block...]
    reduce_scatter x2, waiting for transfers between devices: 58.3 us -> 141 us  [reduce_grads(): mine = lax.psum_scatter(grad_pack, 'dp', scatter_dimension=0, tiled=False)]
    dot_general x18 -> x0, matrix products: 59.2 us -> none  [the longest x6 20.6 us: contract_rows(): lax.dot_general(left_rows, right_rows, (((0,), (0,)), ((), ())), preferre...]
    unnamed x24 -> x2, other arithmetic: 27.8 us -> 0.13 us
    reshape x24 -> x12, local copies, waits for them, and re-layouts: 26.3 us -> 2.19 us  [the longest x2 0.92 us: gathered_params(): wide = tail[:, :3, :first_rows].transpose(1, 0, 2).reshape(3, -1)]
    unnamed x174 -> x57, local copies, waits for them, and re-layouts: 34.6 us -> 13.7 us
    transpose x8, local copies, waits for them, and re-layouts: 20.6 us -> 1.27 us  [the longest x4 0.64 us: gathered_params(): narrow = tail[:, 3:9, :middle_rows].transpose(1, 0, 2).reshape(6, -1)]
    slice x36 -> x31, local copies, waits for them, and re-layouts: 19.9 us -> 6.37 us  [the longest x3 2.32 us: vector_pack(): rows = [device_shards[i][block_number] for i in order]]
  transfers between devices with their start and end apart: 24 -> 24, of which waited for: 15 -> 18; matrix products, arithmetic and copies ran while one was open for 26% -> 5% of each run, Pallas kernels for 0% -> 3%
where the time goes in v2:
time: 524 us; the launch traced here: 515 us
  waiting for transfers between devices  313 us (60%)
  Pallas kernels  83.3 us (16%)
  local copies, waits for them, and re-layouts  50.7 us (10%)
  starting transfers between devices  35.4 us (7%)
  other arithmetic  17.9 us (3%)
  between operations  15.5 us (3%)
    reduce_scatter x2, waiting for transfers between devices, reduce_grads(): mine = lax.psum_scatter(grad_pack, 'dp', scatter_dimension=0, tiled=False)  141 us
    ppermute x12, waiting for transfers between devices, shifted(): lax.ppermute(block, 'seq', [(i, (i + step) % count) for i in range(count)])  89.6 us
    all_gather x2, waiting for transfers between devices, gathered_params(): whole = lax.all_gather(jnp.concatenate([upper, lower, vectors]), 'dp')  62.9 us
    pallas_call x2, Pallas kernels, conv_back(): call(functools.partial(conv_back_kernel, dilation_step), rows, [row_block...  24.6 us
    pallas_call x2, Pallas kernels, convolve(): call(functools.partial(convolve_kernel, dilation_step), rows, [row_block(...  19 us
    ppermute x4, starting transfers between devices, seq_neighbours(): low = lax.ppermute(block[:, block.shape[1] - width:], 'seq', forward)  14.4 us
    pallas_call x2, Pallas kernels, weight_grads(): call(weight_grad_kernel, KER + sizes.folds, [pl.BlockSpec((tokens, hidden...  13.8 us
    unnamed x57, local copies, waits for them, and re-layouts  13.7 us
  transfers between devices with their start and end apart: 24, of which 18 were waited for; matrix products, arithmetic and copies ran while one was open for 5% of the time, Pallas kernels for 3%

profile of v2, /device:TPU:17, one launch (start us, length us, event | category | flops | bytes accessed | tf_op | source)
XLA Modules:
  0.0 515.3 jit_solution(7131535047648199166)
XLA Ops:
  20.1 23.3 %collective-permute-done = bf16[720,160]{1,0:T(8,128)(2,1)S(1)} collective-permute-done((bf16[720,160]{1,0:T(8,128)(2,1)S(1)}, bf16[720,160]{1,0:T(8,128)(2,1)S(1)}, u32[]{:S(2)}, u32[]{:S(2)}) %collective-permute-start) | collective-permute-done | bytes 230432 | tf_op jit(solution)/shard_map/ppermute | solution.py:476
  50.8 6.9 %collective-permute-done.5 = bf16[720,160]{1,0:T(8,128)(2,1)S(1)} collective-permute-done((bf16[720,160]{1,0:T(8,128)(2,1)S(1)}, bf16[720,160]{1,0:T(8,128)(2,1)S(1)}, u32[]{:S(2)}, u32[]{:S(2)}) %collective-permute-start.5) | collective-permute-done | bytes 230432 | tf_op jit(solution)/shard_map/ppermute | solution.py:476
  57.7 22.5 %collective-permute-done.6 = bf16[720,160]{1,0:T(8,128)(2,1)S(1)} collective-permute-done((bf16[720,160]{1,0:T(8,128)(2,1)S(1)}, bf16[720,160]{1,0:T(8,128)(2,1)S(1)}, u32[]{:S(2)}, u32[]{:S(2)}) %collective-permute-start.6) | collective-permute-done | bytes 230432 | tf_op jit(solution)/shard_map/ppermute | solution.py:476
  89.2 10.8 %all-gather.5.cloned.1.call-done = bf16[5888,640]{1,0:T(8,128)(2,1)} async-done(((bf16[736,640]{1,0:T(8,128)(2,1)}), bf16[5888,640]{1,0:T(8,128)(2,1)}) %all-gather.5.cloned.1.call-update) | async-done | bytes 7536656 | tf_op jit(solution)/shard_map/all_gather | solution.py:541
  101.1 52.1 %all-gather.7.cloned.1.call-done = bf16[5888,640]{1,0:T(8,128)(2,1)} async-done(((bf16[736,640]{1,0:T(8,128)(2,1)}), bf16[5888,640]{1,0:T(8,128)(2,1)}) %all-gather.7.cloned.1.call-update) | async-done | bytes 7536656 | tf_op jit(solution)/shard_map/all_gather | solution.py:541
  154.2 5.6 %project.2 = (bf16[512,1280]{1,0:T(8,128)(2,1)S(1)}, f32[512,640]{1,0:T(8,128)S(1)}, bf16[512,640]{1,0:T(8,128)(2,1)S(1)}) custom-call(bf16[512,1280]{1,0:T(8,128)(2,1)S(1)} %bitcast.154, bf16[8,736,640]{2,1,0:T(8,128)(2,1)} %bitcast.170, f32[3,1280]{1,0:T(4,128)S(1)} %reshape.886.wide_ref, f32[6,640]{1,0:T(8,128)S(1)} %reshape.887.narrow_ref), custom_call_target="tpu_custom_call" | custom-call | flops 1677721600 | bytes 7864320 | tf_op jit(solution)/shard_map/project/pallas_call | solution.py:321
  164.0 3.8 collective-permute-start.3
  175.0 9.4 %convolve.2 = (bf16[512,3200]{1,0:T(8,128)(2,1)}, f32[512,640]{1,0:T(8,128)S(1)}, bf16[512,640]{1,0:T(8,128)(2,1)S(1)}, f32[512,1280]{1,0:T(8,128)}) custom-call(bf16[2,128,640]{2,1,0:T(8,128)(2,1)} %collective-permute-done.3.low_ref, bf16[2,256,640]{2,1,0:T(8,128)(2,1)S(1)} %bitcast.165, bf16[2,128,640]{2,1,0:T(8,128)(2,1)} %collective-permute-done.4.high_ref, ...), custom_call_target="tpu_custom_call" | custom-call | flops 2936012800 | bytes 10485760 | tf_op jit(solution)/shard_map/convolve/pallas_call | solution.py:343
  188.0 5.5 %project.3 = (bf16[512,1280]{1,0:T(8,128)(2,1)S(1)}, f32[512,640]{1,0:T(8,128)S(1)}, bf16[512,640]{1,0:T(8,128)(2,1)S(1)}) custom-call(f32[512,1280]{1,0:T(8,128)S(1)} %copy-done, bf16[8,736,640]{2,1,0:T(8,128)(2,1)} %bitcast.187, f32[3,1280]{1,0:T(4,128)S(1)} %reshape.891.wide_ref, f32[6,640]{1,0:T(8,128)S(1)} %reshape.892.narrow_ref), custom_call_target="tpu_custom_call" | custom-call | flops 1677721600 | bytes 7864320 | tf_op jit(solution)/shard_map/project/pallas_call | solution.py:321
  197.8 4.1 collective-permute-start.8
  205.1 7.4 %collective-permute-done.9.high_ref = bf16[2,256,640]{2,1,0:T(8,128)(2,1)} collective-permute-done((bf16[2,256,640]{2,1,0:T(8,128)(2,1)S(1)}, bf16[2,256,640]{2,1,0:T(8,128)(2,1)}, u32[]{:S(2)}, u32[]{:S(2)}) %collective-permute-start.9) | collective-permute-done | bytes 655392 | tf_op jit(solution)/shard_map/ppermute | solution.py:27
  214.4 9.6 %convolve.3 = (bf16[512,3200]{1,0:T(8,128)(2,1)}, f32[512,640]{1,0:T(8,128)S(1)}, bf16[512,640]{1,0:T(8,128)(2,1)S(1)}, bf16[512,1280]{1,0:T(8,128)(2,1)}) custom-call(bf16[2,256,640]{2,1,0:T(8,128)(2,1)} %collective-permute-done.8.low_ref, bf16[2,256,640]{2,1,0:T(8,128)(2,1)S(1)} %bitcast.168, bf16[2,256,640]{2,1,0:T(8,128)(2,1)} %collective-permute-done.9.high_ref, ...), custom_call_target="tpu_custom_call" | custom-call | flops 2936012800 | bytes 10485760 | tf_op jit(solution)/shard_map/convolve/pallas_call | solution.py:343
  224.0 4.9 out_back.2
  234.4 6.9 %weight_grads.3.pack_in_ref = bf16[8,736,640]{2,1,0:T(8,128)(2,1)} custom-call(bf16[512,3200]{1,0:T(8,128)(2,1)S(1)} %copy-done.5, bf16[512,640]{1,0:T(8,128)(2,1)S(1)} %get-tuple-element.57.gv_ref, bf16[512,640]{1,0:T(8,128)(2,1)S(1)} %get-tuple-element.74.act_three_ref, bf16[512,1280]{1,0:T(8,128)(2,1)S(1)} %get-tuple-element.75.short_ref), custom_call_target="tpu_custom_call" | custom-call | flops 2936012800 | bytes 5242880 | tf_op jit(solution)/shard_map/weight_grads/pallas_call | solution.py:403
  246.7 12.3 %conv_back.2 = (bf16[512,640]{1,0:T(8,128)(2,1)S(1)}, f32[512,1280]{1,0:T(8,128)}, f32[8,640]{1,0:T(8,128)S(1)}, f32[8,1280]{1,0:T(8,128)S(1)}) custom-call(bf16[2,256,640]{2,1,0:T(8,128)(2,1)S(1)} %collective-permute-done.10.low_ref, bf16[2,256,640]{2,1,0:T(8,128)(2,1)S(1)} %bitcast.163, bf16[2,256,640]{2,1,0:T(8,128)(2,1)S(1)} %collective-permute-done.11.high_ref, ...), custom_call_target="tpu_custom_call" | custom-call | flops 2936012800 | bytes 10485760 | tf_op jit(solution)/shard_map/conv_back/pallas_call | solution.py:428
  263.1 5.0 out_back.3
  276.2 6.9 %weight_grads.2.pack_in_ref = bf16[8,736,640]{2,1,0:T(8,128)(2,1)} custom-call(bf16[512,3200]{1,0:T(8,128)(2,1)S(1)} %copy-done.4, bf16[512,640]{1,0:T(8,128)(2,1)S(1)} %get-tuple-element.61.gv_ref, bf16[512,640]{1,0:T(8,128)(2,1)S(1)} %copy-done.15, bf16[512,1280]{1,0:T(8,128)(2,1)S(1)} %get-tuple-element.66.short_ref), custom_call_target="tpu_custom_call" | custom-call | flops 2936012800 | bytes 5242880 | tf_op jit(solution)/shard_map/weight_grads/pallas_call | solution.py:403
  283.1 12.3 %conv_back.3 = (bf16[512,640]{1,0:T(8,128)(2,1)S(1)}, f32[512,1280]{1,0:T(8,128)}, f32[8,640]{1,0:T(8,128)S(1)}, f32[8,1280]{1,0:T(8,128)S(1)}) custom-call(bf16[2,128,640]{2,1,0:T(8,128)(2,1)S(1)} %collective-permute-done.12.low_ref, bf16[2,256,640]{2,1,0:T(8,128)(2,1)S(1)} %bitcast.158, bf16[2,128,640]{2,1,0:T(8,128)(2,1)S(1)} %collective-permute-done.13.high_ref, ...), custom_call_target="tpu_custom_call" | custom-call | flops 2936012800 | bytes 10485760 | tf_op jit(solution)/shard_map/conv_back/pallas_call | solution.py:428
  299.7 69.9 %reduce-scatter.5.cloned.1.call-done = bf16[1,736,640]{2,1,0:T(8,128)(2,1)} async-done(((bf16[8,736,640]{2,1,0:T(8,128)(2,1)}), bf16[1,736,640]{2,1,0:T(8,128)(2,1)}) %reduce-scatter.5.cloned.1.call-update) | async-done | bytes 942096 | tf_op jit(solution)/shard_map/reduce_scatter | solution.py:585
  370.3 70.9 %reduce-scatter.3.cloned.1.call-done = bf16[1,736,640]{2,1,0:T(8,128)(2,1)} async-done(((bf16[8,736,640]{2,1,0:T(8,128)(2,1)}), bf16[1,736,640]{2,1,0:T(8,128)(2,1)}) %reduce-scatter.3.cloned.1.call-update) | async-done | bytes 942096 | tf_op jit(solution)/shard_map/reduce_scatter | solution.py:585
  459.5 7.4 %collective-permute-done.14 = bf16[736,160]{0,1:T(8,128)(2,1)S(1)} collective-permute-done((bf16[736,160]{0,1:T(8,128)(2,1)S(1)}, bf16[736,160]{0,1:T(8,128)(2,1)S(1)}, u32[]{:S(2)}, u32[]{:S(2)}) %collective-permute-start.14) | collective-permute-done | bytes 235552 | tf_op jit(solution)/shard_map/ppermute | solution.py:476
  467.0 15.3 %collective-permute-done.15 = bf16[736,160]{0,1:T(8,128)(2,1)S(1)} collective-permute-done((bf16[736,160]{0,1:T(8,128)(2,1)S(1)}, bf16[736,160]{0,1:T(8,128)(2,1)S(1)}, u32[]{:S(2)}, u32[]{:S(2)}) %collective-permute-start.15) | collective-permute-done | bytes 235552 | tf_op jit(solution)/shard_map/ppermute | solution.py:476
  483.4 4.6 collective-permute-done.17
  488.0 9.1 %collective-permute-done.18 = bf16[736,160]{0,1:T(8,128)(2,1)S(1)} collective-permute-done((bf16[736,160]{0,1:T(8,128)(2,1)S(1)}, bf16[736,160]{0,1:T(8,128)(2,1)S(1)}, u32[]{:S(2)}, u32[]{:S(2)}) %collective-permute-start.18) | collective-permute-done | bytes 235552 | tf_op jit(solution)/shard_map/ppermute | solution.py:476
  (294 shorter events, 113.2 us)
Async XLA Ops:
  7.2 92.8 %all-gather.5.cloned.1.call-start = ((), (), s32[]{:S(2)}) async-start(), calls=%async_computation.4 | async-start | bytes 8478720 | tf_op jit(solution)/shard_map/all_gather | solution.py:541
  10.3 33.2 %collective-permute-start.2 = (bf16[720,160]{1,0:T(8,128)(2,1)S(1)}, bf16[720,160]{1,0:T(8,128)(2,1)S(1)}, u32[]{:S(2)}, u32[]{:S(2)}) collective-permute-start(bf16[720,160]{1,0:T(8,128)(2,1)S(1)} %pad_maximum_fusion.1), channel_id=1, source_target_pairs={{0,1},{1,2},{2,3},{3,0},{4,5},{5,6},{6,7},{7,4},{8,9},{9,10},{10,1... | collective-permute-start | bytes 691208 | tf_op jit(solution)/shard_map/ppermute | solution.py:476
  11.6 31.8 %collective-permute-start.1 = (bf16[720,160]{1,0:T(8,128)(2,1)S(1)}, bf16[720,160]{1,0:T(8,128)(2,1)S(1)}, u32[]{:S(2)}, u32[]{:S(2)}) collective-permute-start(bf16[720,160]{1,0:T(8,128)(2,1)S(1)} %pad_maximum_fusion.1), channel_id=1, source_target_pairs={{0,2},{1,3},{2,0},{3,1},{4,6},{5,7},{6,4},{7,5},{8,10},{9,11},{10,... | collective-permute-start | bytes 691208 | tf_op jit(solution)/shard_map/ppermute | solution.py:476
  11.7 31.7 %collective-permute-start = (bf16[720,160]{1,0:T(8,128)(2,1)S(1)}, bf16[720,160]{1,0:T(8,128)(2,1)S(1)}, u32[]{:S(2)}, u32[]{:S(2)}) collective-permute-start(bf16[720,160]{1,0:T(8,128)(2,1)S(1)} %pad_maximum_fusion.1), channel_id=1, source_target_pairs={{0,3},{1,0},{2,1},{3,2},{4,7},{5,4},{6,5},{7,6},{8,11},{9,8},{10,9... | collective-permute-start | bytes 691208 | tf_op jit(solution)/shard_map/ppermute | solution.py:476
  46.7 106.5 %all-gather.7.cloned.1.call-start = ((), (), s32[]{:S(2)}) async-start(), calls=%async_computation.5 | async-start | bytes 8478720 | tf_op jit(solution)/shard_map/all_gather | solution.py:541
  46.8 10.8 %collective-permute-start.5 = (bf16[720,160]{1,0:T(8,128)(2,1)S(1)}, bf16[720,160]{1,0:T(8,128)(2,1)S(1)}, u32[]{:S(2)}, u32[]{:S(2)}) collective-permute-start(bf16[720,160]{1,0:T(8,128)(2,1)S(1)} %pad_maximum_fusion.2), channel_id=1, source_target_pairs={{0,3},{1,0},{2,1},{3,2},{4,7},{5,4},{6,5},{7,6},{8,11},{9,8},{10,9... | collective-permute-start | bytes 691208 | tf_op jit(solution)/shard_map/ppermute | solution.py:476
  49.1 31.2 %collective-permute-start.7 = (bf16[720,160]{1,0:T(8,128)(2,1)S(1)}, bf16[720,160]{1,0:T(8,128)(2,1)S(1)}, u32[]{:S(2)}, u32[]{:S(2)}) collective-permute-start(bf16[720,160]{1,0:T(8,128)(2,1)S(1)} %pad_maximum_fusion.2), channel_id=1, source_target_pairs={{0,1},{1,2},{2,3},{3,0},{4,5},{5,6},{6,7},{7,4},{8,9},{9,10},{10,1... | collective-permute-start | bytes 691208 | tf_op jit(solution)/shard_map/ppermute | solution.py:476
  49.1 31.2 %collective-permute-start.6 = (bf16[720,160]{1,0:T(8,128)(2,1)S(1)}, bf16[720,160]{1,0:T(8,128)(2,1)S(1)}, u32[]{:S(2)}, u32[]{:S(2)}) collective-permute-start(bf16[720,160]{1,0:T(8,128)(2,1)S(1)} %pad_maximum_fusion.2), channel_id=1, source_target_pairs={{0,2},{1,3},{2,0},{3,1},{4,6},{5,7},{6,4},{7,5},{8,10},{9,11},{10,... | collective-permute-start | bytes 691208 | tf_op jit(solution)/shard_map/ppermute | solution.py:476
  86.2 283.4 %reduce-scatter.5.cloned.1.call-start = ((), (), s32[]{:S(2)}) async-start(), calls=%async_computation.3 | async-start | bytes 8478720 | tf_op jit(solution)/shard_map/reduce_scatter | solution.py:585
  161.8 11.3 %collective-permute-start.4 = (bf16[2,128,640]{2,1,0:T(8,128)(2,1)}, bf16[2,128,640]{2,1,0:T(8,128)(2,1)}, u32[]{:S(2)}, u32[]{:S(2)}) collective-permute-start(bf16[2,128,640]{2,1,0:T(8,128)(2,1)} %get-tuple-element.182), channel_id=1, source_target_pairs={{1,0},{2,1},{3,2},{5,4},{6,5},{7,6},{9,8},{10,9},{11,10},{13,12},{... | collective-permute-start | bytes 983048 | tf_op jit(solution)/shard_map/ppermute | solution.py:27
  164.0 11.0 %collective-permute-start.3 = (bf16[2,128,640]{2,1,0:T(8,128)(2,1)}, bf16[2,128,640]{2,1,0:T(8,128)(2,1)}, u32[]{:S(2)}, u32[]{:S(2)}) collective-permute-start(bf16[2,128,640]{2,1,0:T(8,128)(2,1)} %get-tuple-element.183), channel_id=1, source_target_pairs={{0,1},{1,2},{2,3},{4,5},{5,6},{6,7},{8,9},{9,10},{10,11},{12,13},{... | collective-permute-start | bytes 983048 | tf_op jit(solution)/shard_map/ppermute | solution.py:26
  195.7 16.8 %collective-permute-start.9 = (bf16[2,256,640]{2,1,0:T(8,128)(2,1)S(1)}, bf16[2,256,640]{2,1,0:T(8,128)(2,1)}, u32[]{:S(2)}, u32[]{:S(2)}) collective-permute-start(bf16[2,256,640]{2,1,0:T(8,128)(2,1)S(1)} %bitcast.166), channel_id=1, source_target_pairs={{1,0},{2,1},{3,2},{5,4},{6,5},{7,6},{9,8},{10,9},{11,10},{13,12},{... | collective-permute-start | bytes 1966088 | tf_op jit(solution)/shard_map/ppermute | solution.py:27
  197.8 16.6 %collective-permute-start.8 = (bf16[2,256,640]{2,1,0:T(8,128)(2,1)S(1)}, bf16[2,256,640]{2,1,0:T(8,128)(2,1)}, u32[]{:S(2)}, u32[]{:S(2)}) collective-permute-start(bf16[2,256,640]{2,1,0:T(8,128)(2,1)S(1)} %bitcast.167), channel_id=1, source_target_pairs={{0,1},{1,2},{2,3},{4,5},{5,6},{6,7},{8,9},{9,10},{10,11},{12,13},{... | collective-permute-start | bytes 1966088 | tf_op jit(solution)/shard_map/ppermute | solution.py:26
  228.9 15.5 %collective-permute-start.11 = (bf16[2,256,640]{2,1,0:T(8,128)(2,1)S(1)}, bf16[2,256,640]{2,1,0:T(8,128)(2,1)S(1)}, u32[]{:S(2)}, u32[]{:S(2)}) collective-permute-start(bf16[2,256,640]{2,1,0:T(8,128)(2,1)S(1)} %bitcast.161), channel_id=1, source_target_pairs={{1,0},{2,1},{3,2},{5,4},{6,5},{7,6},{9,8},{10,9},{11,10},{13,12},{... | collective-permute-start | bytes 1966088 | tf_op jit(solution)/shard_map/ppermute | solution.py:27
  231.1 15.5 %collective-permute-start.10 = (bf16[2,256,640]{2,1,0:T(8,128)(2,1)S(1)}, bf16[2,256,640]{2,1,0:T(8,128)(2,1)S(1)}, u32[]{:S(2)}, u32[]{:S(2)}) collective-permute-start(bf16[2,256,640]{2,1,0:T(8,128)(2,1)S(1)} %bitcast.162), channel_id=1, source_target_pairs={{0,1},{1,2},{2,3},{4,5},{5,6},{6,7},{8,9},{9,10},{10,11},{12,13},{... | collective-permute-start | bytes 1966088 | tf_op jit(solution)/shard_map/ppermute | solution.py:26
  268.2 14.9 %collective-permute-start.13 = (bf16[2,128,640]{2,1,0:T(8,128)(2,1)S(1)}, bf16[2,128,640]{2,1,0:T(8,128)(2,1)S(1)}, u32[]{:S(2)}, u32[]{:S(2)}) collective-permute-start(bf16[2,128,640]{2,1,0:T(8,128)(2,1)S(1)} %get-tuple-element.180), channel_id=1, source_target_pairs={{1,0},{2,1},{3,2},{5,4},{6,5},{7,6},{9,8},{10,9},{11,10},{13,12},{... | collective-permute-start | bytes 983048 | tf_op jit(solution)/shard_map/ppermute | solution.py:27
  270.5 12.7 %collective-permute-start.12 = (bf16[2,128,640]{2,1,0:T(8,128)(2,1)S(1)}, bf16[2,128,640]{2,1,0:T(8,128)(2,1)S(1)}, u32[]{:S(2)}, u32[]{:S(2)}) collective-permute-start(bf16[2,128,640]{2,1,0:T(8,128)(2,1)S(1)} %get-tuple-element.181), channel_id=1, source_target_pairs={{0,1},{1,2},{2,3},{4,5},{5,6},{6,7},{8,9},{9,10},{10,11},{12,13},{... | collective-permute-start | bytes 983048 | tf_op jit(solution)/shard_map/ppermute | solution.py:26
  299.1 142.1 %reduce-scatter.3.cloned.1.call-start = ((), (), s32[]{:S(2)}) async-start(), calls=%async_computation.2 | async-start | bytes 8478720 | tf_op jit(solution)/shard_map/reduce_scatter | solution.py:585
  451.4 15.6 %collective-permute-start.14 = (bf16[736,160]{0,1:T(8,128)(2,1)S(1)}, bf16[736,160]{0,1:T(8,128)(2,1)S(1)}, u32[]{:S(2)}, u32[]{:S(2)}) collective-permute-start(bf16[736,160]{0,1:T(8,128)(2,1)S(1)} %get-tuple-element.174), channel_id=1, source_target_pairs={{0,2},{1,3},{2,0},{3,1},{4,6},{5,7},{6,4},{7,5},{8,10},{9,11},{10,... | collective-permute-start | bytes 706568 | tf_op jit(solution)/shard_map/ppermute | solution.py:476
  451.7 30.6 %collective-permute-start.15 = (bf16[736,160]{0,1:T(8,128)(2,1)S(1)}, bf16[736,160]{0,1:T(8,128)(2,1)S(1)}, u32[]{:S(2)}, u32[]{:S(2)}) collective-permute-start(bf16[736,160]{0,1:T(8,128)(2,1)S(1)} %get-tuple-element.175), channel_id=1, source_target_pairs={{0,1},{1,2},{2,3},{3,0},{4,5},{5,6},{6,7},{7,4},{8,9},{9,10},{10,1... | collective-permute-start | bytes 706568 | tf_op jit(solution)/shard_map/ppermute | solution.py:476
  452.9 29.9 %collective-permute-start.16 = (bf16[736,160]{0,1:T(8,128)(2,1)S(1)}, bf16[736,160]{0,1:T(8,128)(2,1)S(1)}, u32[]{:S(2)}, u32[]{:S(2)}) collective-permute-start(bf16[736,160]{0,1:T(8,128)(2,1)S(1)} %get-tuple-element.176), channel_id=1, source_target_pairs={{0,3},{1,0},{2,1},{3,2},{4,7},{5,4},{6,5},{7,6},{8,11},{9,8},{10,9... | collective-permute-start | bytes 706568 | tf_op jit(solution)/shard_map/ppermute | solution.py:476
  456.2 31.8 %collective-permute-start.17 = (bf16[736,160]{0,1:T(8,128)(2,1)S(1)}, bf16[736,160]{0,1:T(8,128)(2,1)S(1)}, u32[]{:S(2)}, u32[]{:S(2)}) collective-permute-start(bf16[736,160]{0,1:T(8,128)(2,1)S(1)} %get-tuple-element.177), channel_id=1, source_target_pairs={{0,2},{1,3},{2,0},{3,1},{4,6},{5,7},{6,4},{7,5},{8,10},{9,11},{10,... | collective-permute-start | bytes 706568 | tf_op jit(solution)/shard_map/ppermute | solution.py:476
  459.5 37.6 %collective-permute-start.18 = (bf16[736,160]{0,1:T(8,128)(2,1)S(1)}, bf16[736,160]{0,1:T(8,128)(2,1)S(1)}, u32[]{:S(2)}, u32[]{:S(2)}) collective-permute-start(bf16[736,160]{0,1:T(8,128)(2,1)S(1)} %get-tuple-element.178), channel_id=1, source_target_pairs={{0,1},{1,2},{2,3},{3,0},{4,5},{5,6},{6,7},{7,4},{8,9},{9,10},{10,1... | collective-permute-start | bytes 706568 | tf_op jit(solution)/shard_map/ppermute | solution.py:476
  467.0 30.2 %collective-permute-start.19 = (bf16[736,160]{0,1:T(8,128)(2,1)S(1)}, bf16[736,160]{0,1:T(8,128)(2,1)S(1)}, u32[]{:S(2)}, u32[]{:S(2)}) collective-permute-start(bf16[736,160]{0,1:T(8,128)(2,1)S(1)} %get-tuple-element.179), channel_id=1, source_target_pairs={{0,3},{1,0},{2,1},{3,2},{4,7},{5,4},{6,5},{7,6},{8,11},{9,8},{10,9... | collective-permute-start | bytes 706568 | tf_op jit(solution)/shard_map/ppermute | solution.py:476
  (22 other events, 289.9 us)
Sparse Core Ops, SparseCore 0:
  46.8 53.0 all-gather.4
  102.4 50.7 all-gather.6
  299.2 70.3 reduce-scatter.4
  373.3 67.8 reduce-scatter.2
